TPU v7x, 32 devices: a whole 2x2x4 slice. The times are simulated.
32 devices in a mesh: dp: 8 (over y, x, core), tensor: 4 (over z).
Axes of the slice: x: 2, y: 2, z: 4, core: 2. Of those that a mesh axis runs over, the one named last changes fastest.
Arguments:
- tokens: bfloat16 [16384, 768], P('dp'), may hold values from -6 to 6
- lengths: int32 [32, 8], P('dp'), may hold values from 0 to 256, as said below
- key_mask: int32 [16384], P('dp'), may hold values 0 or 1
- query_weight: bfloat16 [768, 768], P(None, 'tensor'), may hold values from -0.21875 to 0.21875
- query_bias: bfloat16 [768], P('tensor'), may hold values from -3 to 3
- key_weight: bfloat16 [768, 768], P(None, 'tensor'), may hold values from -0.21875 to 0.21875
- value_weight: bfloat16 [768, 768], P(None, 'tensor'), may hold values from -0.21875 to 0.21875
- value_bias: bfloat16 [768], P('tensor'), may hold values from -3 to 3
- output_weight: bfloat16 [768, 768], P('tensor'), may hold values from -0.75 to 0.75
- output_bias: bfloat16 [768], replicated, may hold values from -2 to 2
- first_gain: bfloat16 [768], replicated, may hold values from 0.5 to 1.5
- first_shift: bfloat16 [768], replicated, may hold values from -2 to 2
- inner_weight: bfloat16 [768, 3072], P(None, 'tensor'), may hold values from -0.21875 to 0.21875
- inner_bias: bfloat16 [3072], P('tensor'), may hold values from -3 to 3
- outer_weight: bfloat16 [3072, 768], P('tensor'), may hold values from -0.109375 to 0.109375
- outer_bias: bfloat16 [768], replicated, may hold values from -2 to 2
- second_gain: bfloat16 [768], replicated, may hold values from 0.5 to 1.5
- second_shift: bfloat16 [768], replicated, may hold values from -2 to 2
- cotangent: bfloat16 [16384, 768], P('dp'), may hold values from -6 to 6
Outputs:
- output: bfloat16 [16384, 768], P('dp')
- tokens_grad: bfloat16 [16384, 768], P('dp')
- query_weight_grad: float32 [768, 768], P(None, 'tensor')
- query_bias_grad: float32 [768], P('tensor')
- key_weight_grad: float32 [768, 768], P(None, 'tensor')
- value_weight_grad: float32 [768, 768], P(None, 'tensor')
- value_bias_grad: float32 [768], P('tensor')
- output_weight_grad: float32 [768, 768], P('tensor')
- output_bias_grad: float32 [768], replicated
- first_gain_grad: float32 [768], replicated
- first_shift_grad: float32 [768], replicated
- inner_weight_grad: float32 [768, 3072], P(None, 'tensor')
- inner_bias_grad: float32 [3072], P('tensor')
- outer_weight_grad: float32 [3072, 768], P('tensor')
- outer_bias_grad: float32 [768], replicated
- second_gain_grad: float32 [768], replicated
- second_shift_grad: float32 [768], replicated
Inputs may be any that keep to these rules, and one draw needn't show every extreme that they name: Per bucket, the item lengths sum to at most 512; slots past the live items are pad slots; one item of some bucket has exactly 256 tokens.
All inputs are finite; a program needn't handle non-finite values. No bound on the sum of `key_mask` on one device may be relied on, other than what follows from the above.
Results may differ from a plain program's by a relative error of at most 0.015.
Values may be sent and summed in bfloat16 or wider, within the bound.
No kernel may reach another device: no remote copies, remote signals or barrier semaphores. Data moves between devices by JAX's collectives and lax.ppermute only.
A program may use at most 128 MiB of HBM per device.

v0:
```python
import functools

import jax
import jax.numpy as jnp
from jax import lax
from jax.experimental import pallas as pl
from jax.experimental.pallas import tpu as pltpu
from jax.sharding import PartitionSpec as P

HEAD = 64
BUCKET = 512
ITEMS = 8


negative_fill = -1e30
epsilon = 1e-06
f32 = jnp.float32
bf16 = jnp.bfloat16
VMEM_BYTES = 56 * 1024 * 1024


def dot(left, right):
    return jnp.dot(left, right, preferred_element_type=f32)


def contract_rows(left, right):
    return lax.dot_general(left, right, (((0,), (0,)), ((), ())), preferred_element_type=f32)


def contract_cols(left, right):
    return lax.dot_general(left, right, (((1,), (1,)), ((), ())), preferred_element_type=f32)


def norm_rows(values):
    centred = values - jnp.mean(values, axis=1, keepdims=True)
    inv_scale = lax.rsqrt(jnp.mean(centred * centred, axis=1, keepdims=True) + epsilon)
    return centred * inv_scale, inv_scale


def norm_back(grad_rows, norm_gain, normed, inv_scale):
    scaled = grad_rows * norm_gain
    return inv_scale * (
        scaled
        - jnp.mean(scaled, axis=1, keepdims=True)
        - normed * jnp.mean(scaled * normed, axis=1, keepdims=True)
    )


def column_sum(matrix):
    return jnp.sum(matrix.astype(f32), axis=0, keepdims=True)


def fixed(shape):
    return pl.BlockSpec(shape, lambda *_: (0,) * len(shape))


def cost(microseconds):
    return pl.CostEstimate(
        flops=int(microseconds * 2.5e8),
        bytes_accessed=int(microseconds * 2.5e5),
        transcendentals=0,
    )


def params(axes):
    return pltpu.CompilerParams(
        dimension_semantics=("arbitrary",) * axes, vmem_limit_bytes=VMEM_BYTES
    )


def item_places(lengths_ref, row, shape, axis):
    places = lax.broadcasted_iota(jnp.int32, shape, axis)
    end = jnp.int32(0)
    items = jnp.zeros(shape, jnp.int32)
    for slot in range(ITEMS):
        end = end + lengths_ref[row, slot]
        items = items + (places >= end).astype(jnp.int32)
    return items


def as_column(row):
    return jnp.broadcast_to(row.astype(f32), (8, row.shape[1])).T[:, :1]


def mask_bias(lengths_ref, row, key_mask):
    shape = (BUCKET, BUCKET)
    diagonal = lax.broadcasted_iota(jnp.int32, shape, 0) == lax.broadcasted_iota(
        jnp.int32, shape, 1
    )
    item_row = item_places(lengths_ref, row, (1, BUCKET), 1)
    item_column = item_places(lengths_ref, row, (BUCKET, 1), 0)
    code_column = jnp.where(as_column(key_mask) == 1.0, item_column, -1)
    return jnp.where((code_column == item_row) | diagonal, 0.0, negative_fill).astype(f32)


def attend_forward_kernel(
    lengths_ref, tokens_ref, query_ref, key_ref, value_ref, biases_ref, key_mask_ref, mixed_ref,
):
    mine = query_ref.shape[0]
    rows = tokens_ref[...]
    queries = contract_cols(query_ref[...], rows) + as_column(biases_ref[0:1, :mine])
    queries = (queries.astype(bf16) * HEAD ** (-0.5)).astype(bf16)
    keys = contract_cols(rows, key_ref[...]).astype(bf16)
    values = contract_cols(value_ref[...], rows) + as_column(biases_ref[0:1, mine : 2 * mine])
    values = values.astype(bf16)
    bias = mask_bias(lengths_ref, pl.program_id(0), key_mask_ref[0])
    for head in range(mine // HEAD):
        at = slice(head * HEAD, (head + 1) * HEAD)
        scores = dot(keys[:, at], queries[at]) + bias
        exponent = jnp.exp(scores - jnp.max(scores, axis=0, keepdims=True))
        total = jnp.sum(exponent, axis=0, keepdims=True)
        mixed_ref[0, 0, at] = (dot(values[at], exponent.astype(bf16)) / total).astype(bf16)
    mixed_ref[0, 0, mine:] = biases_ref[...]


def attend_forward(n_z, lengths, tokens, query, key, value, biases, key_mask):
    blocks = lengths.shape[0]
    own = blocks // n_z
    mine, width = key.shape
    whole = (n_z, own, mine + biases.shape[0], BUCKET)
    return pl.pallas_call(
        attend_forward_kernel,
        grid=(blocks,),
        in_specs=[
            pl.BlockSpec(memory_space=pltpu.SMEM),
            pl.BlockSpec((BUCKET, width), lambda b: (b, 0)),
            fixed((mine, width)),
            fixed((mine, width)),
            fixed((mine, width)),
            fixed(biases.shape),
            pl.BlockSpec((1, 1, BUCKET), lambda b: (b, 0, 0)),
        ],
        out_specs=pl.BlockSpec((1, 1) + whole[2:], lambda b: (b // own, b % own, 0, 0)),
        out_shape=jax.ShapeDtypeStruct(whole, bf16),
        compiler_params=params(1),
        name="attend_forward",
        cost_estimate=cost(12),
    )(lengths, tokens, query, key, value, biases, key_mask)


def fetch_units(step, picks, own_ref, halves, units, sems):
    feed_rows = units.shape[2]
    cut = feed_rows // 2

    def copies(number):
        slot = number % 2
        row = pl.multiple_of(picks[number] * feed_rows, 16)
        ends = [
            (own_ref.at[pl.ds(row, feed_rows)], units.at[slot, 0]),
            (halves[number][0], units.at[slot, 1:, :cut]),
            (halves[number][1], units.at[slot, 1:, cut:]),
        ]
        return [
            pltpu.make_async_copy(source, target, sems.at[slot, i])
            for i, (source, target) in enumerate(ends)
        ]

    for number in range(len(halves)):

        @pl.when(step == number)
        def _(number=number):
            if number == 0:
                for copy in copies(0):
                    copy.start()
            if number + 1 < len(halves):
                for copy in copies(number + 1):
                    copy.start()
            for copy in copies(number):
                copy.wait()

    return units.at[lax.rem(step, 2)]


def take_halves(numbers, refs):
    halves, refs = [], list(refs)
    for number in numbers:
        if number == 3:
            halves.append((refs.pop(0), refs.pop(0)))
        else:
            ref = refs.pop(0)
            cut = ref.shape[1] // 2
            halves.append((ref.at[:, :cut], ref.at[:, cut:]))
    return halves, refs


def split_units(units):
    width = units.shape[2] // 2
    return units[:, :, :width].reshape(-1, width), units[:, :, width:].reshape(-1, width)


ANYWHERE = pl.BlockSpec(memory_space=pl.ANY)


def feed_forward_kernel(chunks, first, last, info_ref, *rest):
    def take(count):
        nonlocal rest
        taken, rest = rest[:count], rest[count:]
        return taken

    vectors_ref, bias_ref, own_ref = take(3)
    halves, rest = take_halves([number for _, number in chunks], rest)
    if first:
        tokens_ref, mixed_ref, mixer_ref = take(3)
    else:
        normed_low_ref, start_ref, _, _ = take(4)
    if last:
        lengths_ref, cotangent_ref = take(2)
    hidden_ref, slope_ref = take(2)
    if first:
        normed_low_ref, first_normed_ref, first_scale_ref = take(3)
    if last:
        output_ref, grad_second_ref, grad_outer_ref, sums_ref = take(4)
    else:
        (second_sum,) = take(1)
    units, sems = take(2)
    if last:
        (second_sum,) = take(1)

    step = pl.program_id(0)
    picks = [(info_ref[1] ^ number) * 2 + (info_ref[2] ^ side) for side, number in chunks]
    weights = fetch_units(step, picks, own_ref, halves, units, sems)
    output_bias, first_gain, first_shift, outer_bias, second_gain, second_shift = (
        vectors_ref[i : i + 1, :] for i in range(6)
    )

    @pl.when(step == 0)
    def _():
        if first:
            n_z, own, mine, _ = mixed_ref.shape
            attended = output_bias + jnp.concatenate(
                [
                    sum(
                        contract_rows(mixed_ref[t, b], mixer_ref[t * mine : (t + 1) * mine, :])
                        for t in range(n_z)
                    )
                    for b in range(own)
                ],
                axis=0,
            )
            normed, inv_scale = norm_rows(tokens_ref[...].astype(f32) + attended)
            whole = normed * first_gain + first_shift
            first_normed_ref[...] = normed
            first_scale_ref[...] = inv_scale
            normed_low_ref[...] = whole.astype(bf16)
            second_sum[...] = whole + outer_bias
        else:
            second_sum[...] = start_ref[...]

    inner, outer = split_units(weights)
    inner_pre = contract_cols(normed_low_ref[...], inner) + bias_ref[0]
    normal_cdf = 0.5 + 0.5 * lax.erf(inner_pre * 0.7071067811865476)
    bell = jnp.exp(-0.5 * inner_pre * inner_pre)
    hidden = (inner_pre * normal_cdf).astype(bf16)
    hidden_ref[...] = hidden.T
    slope_ref[...] = (normal_cdf + inner_pre * bell * 0.3989422804014327).astype(bf16)
    second_sum[...] += dot(hidden, outer)

    if last:

        @pl.when(step == pl.num_programs(0) - 1)
        def _():
            normed, inv_scale = norm_rows(second_sum[...])
            blocks = normed.shape[0] // BUCKET
            live = jnp.concatenate(
                [
                    (item_places(lengths_ref, info_ref[0] * blocks + b, (BUCKET, 1), 0) < ITEMS)
                    for b in range(blocks)
                ],
                axis=0,
            ).astype(f32)
            output_ref[...] = ((normed * second_gain + second_shift) * live).astype(bf16)
            grad_final = cotangent_ref[...].astype(f32) * live
            grad_second = norm_back(grad_final, second_gain, normed, inv_scale)
            grad_outer = grad_second.astype(bf16)
            grad_second_ref[...] = grad_second
            grad_outer_ref[...] = grad_outer
            sums_ref[0:1, :] = column_sum(grad_outer)
            sums_ref[1:2, :] = column_sum(grad_final * normed)
            sums_ref[2:3, :] = column_sum(grad_final)


def feed_forward(chunks, info, vectors, biases, own, halves, first=None, going=None, last=None):
    width = vectors.shape[1]
    n_z = halves[0].shape[0] + 1
    feed_rows, twice = own.shape[0] // 8, 2 * width
    rows = first[1].shape[1] * BUCKET if first else going[0].shape[0]
    chunk = n_z * feed_rows
    whole = fixed((rows, width))
    my_rows = pl.BlockSpec((rows, width), lambda j, info: (info[0], 0))
    at = lambda j, info: info[3 + j]
    hidden_spec = pl.BlockSpec((chunk, rows), lambda j, info: (at(j, info), 0))
    slope_spec = pl.BlockSpec((rows, chunk), lambda j, info: (0, at(j, info)))
    in_specs = [
        fixed((8, width)),
        pl.BlockSpec((1, 1, chunk), lambda j, info: (at(j, info), 0, 0)),
        ANYWHERE,
    ] + [ANYWHERE] * len(halves)
    args = [vectors, biases, own] + halves
    shapes = [
        ((8 * chunk, rows), bf16, hidden_spec),
        ((rows, 8 * chunk), bf16, slope_spec),
    ]
    scratch = [
        pltpu.VMEM((2, n_z, feed_rows, twice), bf16),
        pltpu.SemaphoreType.DMA((2, 3)),
    ]
    aliases = {}
    if first:
        tokens, mixed, mixer = first
        mine = width // n_z
        in_specs += [my_rows, fixed((n_z, mixed.shape[1], mine, BUCKET)), fixed(mixer.shape)]
        args += [tokens, mixed, mixer]
        shapes += [
            ((rows, width), bf16, whole),
            ((rows, width), f32, whole),
            ((rows, 1), f32, fixed((rows, 1))),
        ]
    else:
        aliases = {1 + len(args) + 2: 0, 1 + len(args) + 3: 1}
        in_specs += [whole, whole, ANYWHERE, ANYWHERE]
        args += list(going)
    if last:
        in_specs += [pl.BlockSpec(memory_space=pltpu.SMEM), my_rows]
        args += list(last)
        shapes += [
            ((rows, width), bf16, whole),
            ((rows, width), f32, whole),
            ((rows, width), bf16, whole),
            ((8, width), f32, fixed((8, width))),
        ]
        scratch.append(pltpu.VMEM((rows, width), f32))
    else:
        shapes.append(((rows, width), f32, whole))
    info = jnp.concatenate(
        [info, jnp.array([4 * side + number for side, number in chunks], jnp.int32)]
    )
    return pl.pallas_call(
        functools.partial(feed_forward_kernel, chunks, first is not None, last is not None),
        grid_spec=pltpu.PrefetchScalarGridSpec(
            num_scalar_prefetch=1,
            grid=(len(chunks),),
            in_specs=in_specs,
            out_specs=[spec for _, _, spec in shapes],
            scratch_shapes=scratch,
        ),
        out_shape=[jax.ShapeDtypeStruct(shape, kind) for shape, kind, _ in shapes],
        input_output_aliases=aliases,
        compiler_params=params(1),
        name="feed_forward",
        cost_estimate=cost(3 * len(chunks)),
    )(info, *args)


STAY = ((0, 1), (0, 2))
GO = ((2, 3), (1, 3))


def feed_back_kernel(
    keeps, info_ref, grad_outer_ref, normed_low_ref, hidden_ref, slope_ref,
    own_ref, start_ref, *rest,
):
    halves, rest = take_halves(range(4), rest)
    if keeps:
        other_refs, norm_refs, rest = rest[:2], rest[2:5], rest[5:]
        stay_refs, go_refs, rest = rest[0:2], rest[2:4], rest[4:]
        bias_grad_ref, grad_first_ref, grad_attended_ref, sums_ref, units, sems = rest[:6]
        grad_normed_ref = rest[6]
    else:
        *grad_refs, bias_grad_ref, grad_normed_ref, units, sems = rest
    step = pl.program_id(0)
    side = info_ref[2] if keeps else 1 - info_ref[2]
    picks = [(info_ref[1] ^ number) * 2 + side for number in range(4)]
    weights = fetch_units(step, picks, own_ref, halves, units, sems)

    @pl.when(step == 0)
    def _():
        grad_normed_ref[...] = start_ref[...]

    n_z, feed_rows, twice = weights.shape
    width = twice // 2
    inner, outer = split_units(weights)
    grad_outer = grad_outer_ref[...]
    grad_hidden = contract_cols(grad_outer, outer)
    grad_inner = (grad_hidden * slope_ref[...].astype(f32)).astype(bf16)
    outer_grad = dot(hidden_ref[...], grad_outer).reshape(n_z, feed_rows, width)
    inner_grad = contract_rows(grad_inner, normed_low_ref[...]).reshape(n_z, feed_rows, width)
    bias_grad_ref[0] = column_sum(grad_inner)
    grad_normed_ref[...] += dot(grad_inner, inner)

    for number in range(4):

        @pl.when(step == number)
        def _(number=number):
            for track, value in enumerate((inner_grad, outer_grad)):
                at = slice(track * width, (track + 1) * width)
                if keeps:
                    found = value + other_refs[number // 2][0, :, :, at].astype(f32)
                    ref = stay_refs[track] if number in STAY[track] else go_refs[track]
                    ref[0] = found.astype(bf16)
                else:
                    grad_refs[number // 2][0, :, :, at] = value.astype(bf16)

    if keeps:

        @pl.when(step == pl.num_programs(0) - 1)
        def _():
            first_normed_ref, first_scale_ref, vectors_ref = norm_refs
            grad_rows, normed = grad_normed_ref[...], first_normed_ref[...]
            grad_first = norm_back(grad_rows, vectors_ref[1:2, :], normed, first_scale_ref[...])
            grad_attended = grad_first.astype(bf16)
            grad_first_ref[...] = grad_first
            grad_attended_ref[...] = grad_attended
            sums_ref[0:1, :] = column_sum(grad_attended)
            sums_ref[1:2, :] = column_sum(grad_rows * normed)
            sums_ref[2:3, :] = column_sum(grad_rows)


def feed_back(
    info, grad_outer, normed_low, hidden, slope, own, start, units, others=None, norm=None
):
    rows, width = grad_outer.shape
    keeps = others is not None
    count = 4
    feed_rows, twice = own.shape[0] // 8, 2 * width
    n_z = units[0].shape[0] + 1
    chunk = n_z * feed_rows
    flip = 0 if keeps else 1
    columns = pl.BlockSpec((rows, chunk), lambda i, info: (0, 4 * flip + i))
    whole = fixed((rows, width))
    part = (n_z, feed_rows, twice)
    track = (2, n_z, feed_rows, width)
    unit_rows = pl.BlockSpec((chunk, rows), lambda i, info: (4 * flip + i, 0))
    in_specs = [whole, whole, unit_rows, columns, ANYWHERE, whole] + [ANYWHERE] * len(units)
    args = [grad_outer, normed_low, hidden, slope, own, start] + units
    bias_shape = (
        (count, 1, chunk),
        f32,
        pl.BlockSpec((1, 1, chunk), lambda i, info: (i, 0, 0)),
    )
    scratch = [pltpu.VMEM((2,) + part, bf16), pltpu.SemaphoreType.DMA((2, 3))]

    def one(shape, at):
        return pl.BlockSpec((1,) + shape[1:], lambda i, info: (at(i), 0, 0, 0))

    early, late = (lambda i: jnp.minimum(i, 1)), (lambda i: jnp.maximum(i - 2, 0))
    pair = (2,) + part
    if keeps:
        in_specs += [one(pair, early), one(pair, late)]
        in_specs += [whole, fixed((rows, 1)), fixed((8, width))]
        args += list(others) + list(norm)
        slow, slower = (lambda i: i // 2), (lambda i: jnp.maximum(i - 1, 0) // 2)
        shapes = [(track, bf16, one(track, at)) for at in (early, slow, late, slower)] + [
            bias_shape,
            ((rows, width), f32, whole),
            ((rows, width), bf16, whole),
            ((8, width), f32, fixed((8, width))),
        ]
        scratch.append(pltpu.VMEM((rows, width), f32))
    else:
        shapes = [
            (pair, bf16, one(pair, early)),
            (pair, bf16, one(pair, late)),
            bias_shape,
            ((rows, width), f32, whole),
        ]
    return pl.pallas_call(
        functools.partial(feed_back_kernel, keeps),
        grid_spec=pltpu.PrefetchScalarGridSpec(
            num_scalar_prefetch=1,
            grid=(count,),
            in_specs=in_specs,
            out_specs=[spec for _, _, spec in shapes],
            scratch_shapes=scratch,
        ),
        out_shape=[jax.ShapeDtypeStruct(shape, kind) for shape, kind, _ in shapes],
        compiler_params=params(1),
        name="feed_back_own" if keeps else "feed_back",
        cost_estimate=cost(3 * count),
    )(info, *args)


def finish_feed_kernel(core_ref, own_ref, other_ref, inner_ref, outer_ref, inner_rows):
    places, count, twice = own_ref.shape
    width = twice // 2
    for source, side in ((own_ref, core_ref[0]), (other_ref, 1 - core_ref[0])):
        for place in range(places):
            row = pl.multiple_of((2 * place + side) * count, 16)
            inner_rows[pl.ds(row, count), :] = source[place, :, :width].astype(f32)
            outer_ref[pl.ds(row, count), :] = source[place, :, width:].astype(f32)
    inner_ref[...] = inner_rows[...].T


def finish_feed(core, own, other):
    places, count, twice = own.shape
    shape = (2 * places * count, twice // 2)
    inner_shape = (shape[1], shape[0])
    return pl.pallas_call(
        finish_feed_kernel,
        grid_spec=pltpu.PrefetchScalarGridSpec(
            num_scalar_prefetch=1,
            grid=(1,),
            in_specs=[fixed(own.shape), fixed(other.shape)],
            out_specs=[fixed(inner_shape), fixed(shape)],
            scratch_shapes=[pltpu.VMEM(shape, f32)],
        ),
        out_shape=[
            jax.ShapeDtypeStruct(inner_shape, f32),
            jax.ShapeDtypeStruct(shape, f32),
        ],
        compiler_params=params(1),
        name="finish_feed",
        cost_estimate=cost(5),
    )(core, own, other)


def copy_kernel(from_ref, to_ref):
    to_ref[...] = from_ref[...]


def copied(array):
    block = pl.BlockSpec((BUCKET, array.shape[1]), lambda i: (i, 0))
    return pl.pallas_call(
        copy_kernel,
        grid=(array.shape[0] // BUCKET,),
        in_specs=[block],
        out_specs=block,
        out_shape=jax.ShapeDtypeStruct(array.shape, array.dtype),
        compiler_params=params(1),
        name="copied",
        cost_estimate=cost(0.5),
    )(array)


def project_kernel(
    place_ref, tokens_ref, own_ref, remote_ref, biases_ref, query_ref, key_ref, value_ref
):
    rows = tokens_ref[...]
    width = rows.shape[1]
    weights = jnp.where(pl.program_id(1) == 0, own_ref[...], remote_ref[0])
    queries = contract_cols(weights[:, :width], rows) + as_column(biases_ref[0, 0:1, :])
    query_ref[...] = (queries.astype(bf16) * HEAD ** (-0.5)).astype(bf16)
    key_ref[...] = contract_cols(weights[:, width : 2 * width], rows).astype(bf16)
    values = contract_cols(weights[:, 2 * width :], rows) + as_column(biases_ref[0, 1:2, :])
    value_ref[...] = values.astype(bf16)


def project(place, tokens, own, remote, biases, buckets):
    width = tokens.shape[1]
    mine = own.shape[0]
    n_z = width // mine
    there = lambda s, place: lax.rem(place[0] + n_z - s, n_z)
    out = pl.BlockSpec((None, mine, BUCKET), lambda b, s, place: (b, there(s, place), 0))
    return pl.pallas_call(
        project_kernel,
        grid_spec=pltpu.PrefetchScalarGridSpec(
            num_scalar_prefetch=1,
            grid=(buckets, n_z),
            in_specs=[
                pl.BlockSpec((BUCKET, width), lambda b, s, place: (place[0] * buckets + b, 0)),
                fixed(own.shape),
                pl.BlockSpec(
                    (1, mine, 3 * width), lambda b, s, place: (jnp.maximum(s - 1, 0), 0, 0)
                ),
                pl.BlockSpec((1, 8, mine), lambda b, s, place: (there(s, place), 0, 0)),
            ],
            out_specs=[out] * 3,
        ),
        out_shape=[jax.ShapeDtypeStruct((buckets, width, BUCKET), bf16)] * 3,
        compiler_params=params(2),
        name="project",
        cost_estimate=cost(5),
    )(place, tokens, own, remote, biases)


def attend_back_kernel(
    place_ref, lengths_ref, grad_attended_ref, grad_first_ref, own_ref, remote_ref, mixer_ref,
    query_ref, key_ref, value_ref, key_mask_ref,
    grads_ref, tokens_grad_ref, sums_ref,
    bias, grad_mixed_t, whole, weights, mixer, sems,
):
    pair = pl.program_id(1)
    pairs, width = whole.shape[1], weights.shape[0]
    mine = own_ref.shape[0]
    n_z = width // mine

    def fetches():
        ends = [(mixer_ref, mixer)]
        for s in range(n_z):
            row = pl.multiple_of(lax.rem(place_ref[0] + n_z - s, n_z) * mine, 16)
            source = own_ref if s == 0 else remote_ref.at[s - 1]
            ends.append((source, weights.at[pl.ds(row, mine)]))
        return [
            pltpu.make_async_copy(source, target, sems.at[i])
            for i, (source, target) in enumerate(ends)
        ]

    @pl.when(pair == 0)
    def _():
        for fetch in fetches():
            fetch.start()
        row = place_ref[0] * pl.num_programs(0) + pl.program_id(0)
        bias[...] = mask_bias(lengths_ref, row, key_mask_ref[0])
        for fetch in fetches():
            fetch.wait()
        grad_mixed_t[...] = contract_cols(mixer[...], grad_attended_ref[...]).astype(bf16)

    queries, keys_t = query_ref[...], key_ref[...]
    keys, values = keys_t.T, value_ref[...].T
    start = pl.multiple_of(pair * keys.shape[1], 128)
    grad_mixed = grad_mixed_t[pl.ds(start, keys.shape[1]), :]
    grad_queries, grad_keys, grad_values = [], [], []
    for head in range(keys.shape[1] // HEAD):
        at = slice(head * HEAD, (head + 1) * HEAD)
        scores = dot(keys[:, at], queries[at]) + bias[...]
        exponent = jnp.exp(scores - jnp.max(scores, axis=0, keepdims=True))
        probs = exponent * (1.0 / jnp.sum(exponent, axis=0, keepdims=True))
        grad_probs = dot(values[:, at], grad_mixed[at])
        shift = jnp.sum(probs * grad_probs, axis=0, keepdims=True)
        grad_scores = (probs * (grad_probs - shift)).astype(bf16)
        grad_values.append(contract_cols(probs.astype(bf16), grad_mixed[at]))
        grad_keys.append(contract_cols(grad_scores, queries[at]))
        grad_queries.append(dot(keys_t[at], grad_scores) * HEAD ** (-0.5))
    query_t = jnp.concatenate(grad_queries, axis=0).astype(bf16)
    found = (
        query_t.T,
        jnp.concatenate(grad_keys, axis=1).astype(bf16),
        jnp.concatenate(grad_values, axis=1).astype(bf16),
    )
    for number, grad in enumerate(found):
        grads_ref[number, 0] = query_t if number == 0 else grad.T
        whole[number, pair] = grad
    sums_ref[0, 0:1, :] = column_sum(found[0])
    sums_ref[0, 1:2, :] = column_sum(found[2])

    @pl.when(pair == pl.num_programs(1) - 1)
    def _():
        total = grad_first_ref[...]
        for number in range(3):
            grad = jnp.concatenate([whole[number, i] for i in range(pairs)], axis=1)
            total += dot(grad, weights[:, number * width : (number + 1) * width])
        tokens_grad_ref[...] = total.astype(bf16)


def attend_back(
    place, lengths, grad_attended, grad_first, own, remote, mixer, queries, keys, values, key_mask
):
    rows, width = grad_attended.shape
    blocks = rows // BUCKET
    pair = 2 * HEAD
    by_bucket = pl.BlockSpec((BUCKET, width), lambda b, h, place: (b, 0))
    by_pair = pl.BlockSpec((None, pair, BUCKET), lambda b, h, place: (b, h, 0))
    return pl.pallas_call(
        attend_back_kernel,
        grid_spec=pltpu.PrefetchScalarGridSpec(
            num_scalar_prefetch=1,
            grid=(blocks, width // pair),
            in_specs=[
                pl.BlockSpec(memory_space=pltpu.SMEM),
                by_bucket,
                by_bucket,
                ANYWHERE,
                ANYWHERE,
                ANYWHERE,
                by_pair,
                by_pair,
                by_pair,
                pl.BlockSpec((1, 1, BUCKET), lambda b, h, place: (place[0] * blocks + b, 0, 0)),
            ],
            out_specs=[
                pl.BlockSpec((3, 1, pair, BUCKET), lambda b, h, place: (0, b, h, 0)),
                by_bucket,
                pl.BlockSpec((1, 8, pair), lambda b, h, place: (b, 0, h)),
            ],
            scratch_shapes=[
                pltpu.VMEM((BUCKET, BUCKET), f32),
                pltpu.VMEM((width, BUCKET), bf16),
                pltpu.VMEM((3, width // pair, BUCKET, pair), bf16),
                pltpu.VMEM((width, own.shape[1]), bf16),
                pltpu.VMEM(mixer.shape, bf16),
                pltpu.SemaphoreType.DMA((1 + width // own.shape[0],)),
            ],
        ),
        out_shape=[
            jax.ShapeDtypeStruct((3, blocks, width, BUCKET), bf16),
            jax.ShapeDtypeStruct((rows, width), bf16),
            jax.ShapeDtypeStruct((blocks, 8, width), f32),
        ],
        compiler_params=params(2),
        name="attend_back",
        cost_estimate=cost(20),
    )(
        place, lengths, grad_attended, grad_first, own, remote, mixer, queries, keys, values, key_mask
    )


def attention_grads_kernel(
    n_places, adds, info_ref, grads_ref, mixed_ref, tokens_ref, grad_attended_ref, *rest
):
    if adds:
        other_refs, small_ref, rest = rest[:n_places], rest[n_places], rest[n_places + 1 :]
    out_refs, whole = rest[:-1], rest[-1]
    step = pl.program_id(0)
    which = info_ref[step]
    n_z, buckets, mine, _ = mixed_ref.shape
    count = mine // n_places

    @pl.when(which < 3)
    def _():
        whole[...] = sum(
            dot(grads_ref[0, b], tokens_ref[b * BUCKET : (b + 1) * BUCKET, :])
            for b in range(buckets)
        ).astype(bf16)

    @pl.when(which == 3)
    def _():
        for t in range(n_z):
            whole[t * mine : (t + 1) * mine, :] = sum(
                dot(mixed_ref[t, b], grad_attended_ref[b * BUCKET : (b + 1) * BUCKET, :])
                for b in range(buckets)
            ).astype(bf16)

    for number in range(n_places):
        for s in range(n_z):
            start = lax.rem(info_ref[2] + s, n_z) * mine + (info_ref[3] ^ number) * count
            value = whole[pl.ds(pl.multiple_of(start, 16), count), :]
            if adds:
                value = value.astype(f32) + other_refs[number][s, 0].astype(f32)
                row = (2 * s + step) * count
                out_refs[number][pl.ds(pl.multiple_of(row, 16), count), :] = value.astype(bf16)
            else:
                out_refs[number][s, 0] = value

    if adds:
        for number in range(n_places):
            out_refs[number][2 * n_z * count :, :] = small_ref[...]


def attention_grads(n_places, info, grads, mixed, tokens, grad_attended, other=None, small=None):
    rows, width = grad_attended.shape
    n_z, buckets = mixed.shape[:2]
    mine = width // n_z
    count = mine // n_places
    by_step = pl.BlockSpec((n_z, 1, count, width), lambda i, info: (0, i, 0, 0))
    in_specs = [
        pl.BlockSpec(
            (1, buckets, width, BUCKET), lambda i, info: (jnp.minimum(info[i], 2), 0, 0, 0)
        ),
        fixed((n_z, buckets, mine, BUCKET)),
        pl.BlockSpec((rows, width), lambda i, info: (info[2], 0)),
        fixed((rows, width)),
    ]
    args = [grads, mixed, tokens, grad_attended]
    if other is None:
        shapes = [((n_z, 2, count, width), by_step)] * n_places
    else:
        in_specs += [by_step] * n_places + [fixed(small.shape)]
        args += list(other) + [small]
        flat = (2 * n_z * count + small.shape[0], width)
        shapes = [(flat, fixed(flat))] * n_places
    return pl.pallas_call(
        functools.partial(attention_grads_kernel, n_places, other is not None),
        grid_spec=pltpu.PrefetchScalarGridSpec(
            num_scalar_prefetch=1,
            grid=(2,),
            in_specs=in_specs,
            out_specs=[spec for _, spec in shapes],
            scratch_shapes=[pltpu.VMEM((width, width), bf16)],
        ),
        out_shape=[jax.ShapeDtypeStruct(shape, bf16) for shape, _ in shapes],
        compiler_params=params(1),
        name="attention_grads",
        cost_estimate=cost(0.5),
    )(info, *args)


def together(*values):
    return lax.optimization_barrier(values)


def add(first, *others):
    total = first.astype(f32)
    for other in others:
        total = total + other.astype(f32)
    return total.astype(bf16)


class Plane:
    def __init__(self, n_dp, n_z):
        self.n_dp, self.n_z = n_dp, n_z
        self.n_group = min(n_dp, 8)
        self.n_places = self.n_group // 2
        self.dp = lax.axis_index("dp")
        self.z = lax.axis_index("tensor")
        self.index = lax.rem(self.dp, self.n_group)
        self.core = self.index & 1
        self.place = self.index >> 1

    def swap(self, array, bits):
        return lax.ppermute(array, "dp", [(i, i ^ bits) for i in range(self.n_dp)])

    def shift(self, array, by):
        n = self.n_z
        return lax.ppermute(array, "tensor", [(i, (i + by) % n) for i in range(n)])

    def gather(self, piece):
        if self.n_dp == self.n_group:
            whole = lax.all_gather(piece, ("tensor", "dp"))
            return whole.reshape((self.n_z, self.n_group) + piece.shape)
        groups = [
            list(range(i, i + self.n_group)) for i in range(0, self.n_dp, self.n_group)
        ]
        line = lax.all_gather(piece, "tensor")
        return lax.all_gather(line, "dp", axis=1, axis_index_groups=groups)

    def turned(self, array):
        bit = 1
        while bit < self.n_group:
            lead = array.reshape((-1, 2, bit) + array.shape[1:])
            array = jnp.where((self.index & bit) != 0, lead[:, ::-1], lead).reshape(array.shape)
            bit *= 2
        return array

    def to_places(self, parts):
        return [self.swap(parts[number], 2 * number) for number in range(1, self.n_places)]

    def from_places(self, own, arrived):
        found = jnp.stack([own] + arrived)
        bit = 1
        while bit < self.n_places:
            lead = found.reshape((-1, 2, bit) + own.shape)
            flipped = lead[:, ::-1]
            found = jnp.where((self.place & bit) != 0, flipped, lead).reshape(found.shape)
            bit *= 2
        return found

    def by_core(self, own, other):
        return jnp.where(
            self.core == 1, jnp.stack([other, own]), jnp.stack([own, other])
        )

    def over_groups(self, array):
        bit = self.n_group
        while bit < self.n_dp:
            array = add(array, self.swap(array, bit))
            bit *= 2
        return array


def on_device(
    n_dp,
    n_z,
    tokens,
    lengths,
    key_mask,
    query_weight,
    query_bias,
    key_weight,
    value_weight,
    value_bias,
    output_weight,
    output_bias,
    first_gain,
    first_shift,
    inner_weight,
    inner_bias,
    outer_weight,
    outer_bias,
    second_gain,
    second_shift,
    cotangent,
):
    width = tokens.shape[1]
    mine = query_weight.shape[1]
    units = inner_weight.shape[1]
    all_rows = tokens.shape[0]
    all_blocks = all_rows // BUCKET
    rows = all_rows // n_z
    plane = Plane(n_dp, n_z)
    z, core, place, index = plane.z, plane.core, plane.place, plane.index
    n_places = plane.n_places
    others = range(1, n_z)

    feed_rows = units // plane.n_group
    head_rows = mine // plane.n_group
    mixer_count = width // plane.n_group
    piece = jnp.concatenate(
        [
            lax.dynamic_slice_in_dim(inner_weight, index * feed_rows, feed_rows, 1).T,
            lax.dynamic_slice_in_dim(outer_weight, index * feed_rows, feed_rows, 0),
        ],
        axis=1,
    )
    line = [plane.shift(piece, s) for s in others]

    mixer = plane.gather(
        lax.dynamic_slice_in_dim(output_weight, index * head_rows, head_rows, 0)
    ).reshape(width, width)
    query_t, key_t, value_t = query_weight.T, key_weight.T, value_weight.T

    key_mask_rows = key_mask.reshape(all_blocks, 1, BUCKET)
    bias_row = jnp.concatenate([query_bias, value_bias, inner_bias])
    bias_rows = jnp.pad(bias_row, (0, 16 * BUCKET - bias_row.shape[0])).reshape(16, BUCKET)
    place_z = z.reshape(1)
    mixed = attend_forward(
        n_z, lengths, tokens, query_t, key_t, value_t, bias_rows, key_mask_rows
    )
    mixed, line = together(mixed, line)

    near = jnp.stack(line)
    by_x, by_y = plane.swap(near, 2), plane.swap(near, 4)
    mixed, near = together(mixed, near)
    mixed = lax.all_to_all(mixed, "tensor", 0, 0)
    own_units = jnp.concatenate([inner_weight.T, outer_weight], axis=1)

    attention_own = jnp.concatenate([query_t, key_t, value_t], axis=1)
    attention_piece = lax.dynamic_slice_in_dim(attention_own, index * head_rows, head_rows, 0)
    attention_line = [plane.shift(attention_piece, s) for s in others]
    biases = mixed[:, 0, mine:].reshape(n_z, -1)[:, : bias_row.shape[0]].astype(f32)
    head_biases = jnp.pad(
        jnp.stack([biases[:, :mine], biases[:, mine : 2 * mine]], axis=1), ((0, 0), (0, 6), (0, 0))
    )
    inner_biases = biases[:, 2 * mine :]
    inner_biases = jnp.concatenate(
        [
            lax.dynamic_slice_in_dim(inner_biases, lax.rem(z + n_z - s, n_z), 1, 0)
            for s in range(n_z)
        ],
        axis=0,
    )
    inner_biases = inner_biases.reshape(n_z, plane.n_group, feed_rows).transpose(1, 0, 2)
    inner_biases = plane.turned(inner_biases).reshape(n_places, 2, 1, n_z * feed_rows)
    inner_biases = inner_biases.transpose(1, 0, 2, 3).reshape(plane.n_group, 1, -1)
    vectors = jnp.stack(
        [output_bias, first_gain, first_shift, outer_bias, second_gain, second_shift]
        + [jnp.zeros_like(output_bias)] * 2
    ).astype(f32)

    info = jnp.stack([z, place, core])
    shared_args = (info, vectors, inner_biases, own_units)
    cut = feed_rows // 2
    far = [plane.swap(by_x[:, :cut], 4), plane.swap(by_y[:, cut:], 2)]
    near_there, x_there, y_there, mixer, attention_line = together(
        near, by_x, by_y, mixer, attention_line
    )
    send = [plane.swap(units_of, 1) for units_of in (near_there, x_there, y_there)]
    attention_line = jnp.stack(attention_line)
    attention_swaps = plane.to_places([attention_line] * n_places)
    hidden, slope, normed_low, first_normed, first_scale, second_sum = feed_forward(
        ((0, 0), (0, 1), (0, 2), (1, 0), (1, 1), (1, 2)),
        *shared_args,
        [near, by_x, by_y] + send,
        first=(tokens, mixed, mixer),
    )
    second_sum, far, attention_swaps = together(second_sum, far, attention_swaps)
    attention_half = plane.from_places(attention_line, attention_swaps)
    attention_other = plane.swap(attention_half, 1)
    far_send = [plane.swap(half, 1) for half in far]
    keep = [near, by_x, by_y] + far
    send = send + far_send
    hidden, slope, my_output, grad_second, grad_outer, second_sums = feed_forward(
        ((0, 3), (1, 3)), *shared_args, far + far_send,
        going=(normed_low, second_sum, hidden, slope), last=(lengths, cotangent),
    )
    output = lax.all_gather(my_output, "tensor", axis=0, tiled=True)

    grad_outer, attention_other = together(grad_outer, attention_other)

    shared_args = (info, grad_outer, normed_low, hidden, slope, own_units)
    sent_early, sent_late, bias_sent, grad_normed = feed_back(*shared_args, grad_second, send)
    other = [plane.swap(sent_early, 1), plane.swap(sent_late, 1)]
    attention_remote = plane.by_core(attention_half, attention_other)
    attention_remote = attention_remote.transpose(2, 1, 0, 3, 4).reshape(n_z - 1, mine, 3 * width)
    projected = project(
        place_z, tokens, attention_own, attention_remote, head_biases, rows // BUCKET
    )
    projected, other = together(projected, other)
    (
        inner_stay, outer_stay, inner_go, outer_go, bias_kept, grad_first, grad_attended, first_sums
    ) = feed_back(
        *shared_args, grad_normed, keep, other,
        (first_normed, first_scale, vectors),
    )
    inner_came, outer_came = plane.swap(inner_go, 4), plane.swap(outer_go, 2)
    bias_grads = jnp.stack(
        [bias_kept[:, 0], bias_sent[:, 0]], axis=1
    )
    inner_bias_grad = plane.turned(bias_grads.reshape(plane.n_group, n_z, feed_rows))
    inner_bias_grad = inner_bias_grad.transpose(1, 0, 2)
    inner_bias_grad = jnp.concatenate(
        [
            sum(
                jnp.where(lax.rem(z - t + n_z, n_z) == s, inner_bias_grad[s : s + 1], 0.0)
                for s in range(n_z)
            )
            for t in range(n_z)
        ],
        axis=0,
    ).reshape(n_z, units)

    grads, my_tokens_grad, back_sums = attend_back(
        place_z, lengths, grad_attended, grad_first, attention_own, attention_remote, mixer,
        *projected, key_mask_rows,
    )
    grads, inner_came, outer_came, output = together(grads, inner_came, outer_came, output)
    inner_on, outer_on = (
        plane.swap(add(inner_stay[1], inner_came[1]), 2),
        plane.swap(add(outer_stay[1], outer_came[1]), 4),
    )
    tokens_grad = lax.all_gather(my_tokens_grad, "tensor", axis=0, tiled=True)

    def weight_grads(side, other=None, small=None):
        info = jnp.stack([2 * side, 2 * side + 1, z, place])
        return attention_grads(
            n_places, info, grads, mixed, tokens, grad_attended, other, small
        )

    sent = weight_grads(1 - core)
    sent, inner_on, outer_on, back_sums, first_sums, second_sums, inner_bias_grad = together(
        sent, inner_on, outer_on, back_sums, first_sums, second_sums, inner_bias_grad
    )
    other = [plane.swap(part, 1) for part in sent]

    small = jnp.concatenate(
        [first_sums[:3], second_sums[:3], inner_bias_grad, jnp.sum(back_sums, axis=0)[:2]], axis=0
    )
    small = jnp.pad(small, ((0, -small.shape[0] % 16), (0, 0))).astype(bf16)
    small_rows = small.shape[0]

    small = add(small, plane.swap(small, 1))
    kept = list(weight_grads(core, other, small))
    arrived = plane.to_places(kept)
    feed_parts = [
        jnp.concatenate(
            [
                add(inner_stay[0, s], inner_came[0, s], inner_on[s]),
                add(outer_stay[0, s], outer_came[0, s], outer_on[s]),
            ],
            axis=1,
        )
        for s in range(n_z)
    ]
    feed_line = [plane.shift(feed_parts[s], -s) for s in others]
    output = copied(output)
    arrived, output = together(arrived, output)
    small = add(small, *[a[-small_rows:] for a in arrived])
    count = 2 * mine // n_places
    attention_parts = [
        add(*[a[s * count : (s + 1) * count] for a in [kept[0]] + arrived]) for s in range(n_z)
    ]
    attention_line = [
        plane.shift(jnp.concatenate([attention_parts[s], small], axis=0), s) for s in others
    ]
    feed_total = plane.over_groups(add(feed_parts[0], *feed_line))
    feed_arrived = plane.to_places([feed_total] * n_places)
    tokens_grad = copied(tokens_grad)
    attention_line, feed_arrived, tokens_grad = together(
        attention_line, feed_arrived, tokens_grad
    )
    attention_total = plane.over_groups(
        add(attention_parts[0], *[a[:count] for a in attention_line])
    )
    small = plane.over_groups(add(small, *[a[count:] for a in attention_line])).astype(f32)
    arrived = plane.to_places([attention_total] * n_places)
    feed_half = plane.from_places(feed_total, feed_arrived)
    feed_other = plane.swap(feed_half, 1)
    inner_grad, outer_grad = finish_feed(core.reshape(1), feed_half, feed_other)
    inner_bias_sum = lax.dynamic_slice_in_dim(small, 6 + z, 1, 0)[0]
    head_sums = lax.dynamic_slice_in_dim(small[6 + n_z : 8 + n_z], z * mine, mine, 1)
    arrived, inner_grad, outer_grad, small, inner_bias_sum, head_sums = together(
        arrived, inner_grad, outer_grad, small, inner_bias_sum, head_sums
    )
    attention_half = plane.from_places(attention_total, arrived)
    attention_other = plane.swap(attention_half, 1)
    grad_list = plane.by_core(attention_half, attention_other)
    grad_list = grad_list.reshape(2, n_places, 2, mine // n_places, width)
    grad_list = grad_list.transpose(0, 2, 1, 3, 4).reshape(4, mine, width)

    shared = small[:6]

    return (
        output,
        tokens_grad,
        grad_list[0].T.astype(f32),
        head_sums[0],
        grad_list[1].T.astype(f32),
        grad_list[2].T.astype(f32),
        head_sums[1],
        grad_list[3].astype(f32),
        shared[0],
        shared[1],
        shared[2],
        inner_grad,
        inner_bias_sum,
        outer_grad,
        shared[3],
        shared[4],
        shared[5],
    )


def solution(mesh):
    n_dp, n_z = mesh.shape["dp"], mesh.shape["tensor"]
    in_specs = (
        P("dp", None),
        P("dp", None),
        P("dp"),
        P(None, "tensor"),
        P("tensor"),
        P(None, "tensor"),
        P(None, "tensor"),
        P("tensor"),
        P("tensor", None),
        P(),
        P(),
        P(),
        P(None, "tensor"),
        P("tensor"),
        P("tensor", None),
        P(),
        P(),
        P(),
        P("dp", None),
    )
    out_specs = (
        P("dp", None),
        P("dp", None),
        P(None, "tensor"),
        P("tensor"),
        P(None, "tensor"),
        P(None, "tensor"),
        P("tensor"),
        P("tensor", None),
        P(),
        P(),
        P(),
        P(None, "tensor"),
        P("tensor"),
        P("tensor", None),
        P(),
        P(),
        P(),
    )

    def program(*args):
        return on_device(n_dp, n_z, *args)

    return jax.shard_map(
        program, mesh=mesh, in_specs=in_specs, out_specs=out_specs, check_vma=False
    )
```

profile of v0, /device:TPU:9, one launch (start us, length us, event | category | flops | bytes accessed | tf_op | source)
XLA Modules:
  0.0 314.6 jit_solution(3616615500440324600)
XLA Ops:
  15.1 11.8 %attend_forward.1 = bf16[4,1,208,512]{3,2,1,0:T(8,128)(2,1)} custom-call(s32[4,8]{1,0:T(4,128)} %lengths_ref.3, bf16[2048,768]{1,0:T(8,128)(2,1)} %tokens_ref.7, bf16[192,768]{1,0:T(8,128)(2,1)} %bitcast.169, bf16[192,768]{1,0:T(8,128)(2,1)} %bitcast.171, bf16[192,768]{1,0:T(8,128)(2,1)} %bitcast.173, bf16[16,512]{1,0:T(8,128)(2,1)} %reshape.149.biases_ref, ...), custom_call_target="tpu_custom_call" | custom-call | flops 3000000000 | bytes 3000000 | tf_op jit(solution)/shard_map/attend_forward/pallas_call | solution.py:121
  27.0 9.6 %collective-permute-done.1 = bf16[96,1536]{1,0:T(8,128)(2,1)S(1)} collective-permute-done((bf16[96,1536]{1,0:T(8,128)(2,1)S(1)}, bf16[96,1536]{1,0:T(8,128)(2,1)S(1)}, u32[]{:S(2)}, u32[]{:S(2)}) %collective-permute-start.1) | collective-permute-done | bytes 294944 | tf_op jit(solution)/shard_map/ppermute | solution.py:803
  36.6 2.9 collective-permute-done.2
  40.6 3.5 %all-to-all-start = ((bf16[4,1,208,512]{3,2,1,0:T(8,128)(2,1)}), bf16[4,1,208,512]{3,2,1,0:T(8,128)(2,1)S(1)}, u32[]{:S(2)}, u32[]{:S(2)}) async-start(bf16[4,1,208,512]{3,2,1,0:T(8,128)(2,1)} %attend_forward.1), calls=%async_computation | async-start | bytes 1703936 | tf_op jit(solution)/shard_map/all_to_all | solution.py:912
  52.0 2.8 pad_maximum_fusion.rest_2_.own_ref
  54.8 11.6 %collective-permute-done.3.rest_4_.rest_1_ = bf16[3,96,1536]{2,1,0:T(8,128)(2,1)} collective-permute-done((bf16[3,96,1536]{2,1,0:T(8,128)(2,1)}, bf16[3,96,1536]{2,1,0:T(8,128)(2,1)}, u32[]{:S(2)}, u32[]{:S(2)}) %collective-permute-start.3) | collective-permute-done | bytes 884768 | tf_op jit(solution)/shard_map/ppermute | solution.py:799
  72.6 2.9 collective-permute-done.6
  86.8 15.7 %feed_forward.2 = (bf16[3072,512]{1,0:T(8,128)(2,1)}, bf16[512,3072]{1,0:T(8,128)(2,1)}, bf16[512,768]{1,0:T(8,128)(2,1)}, f32[512,768]{1,0:T(8,128)}, f32[512,1]{1,0:T(8,128)}, /*index=5*/f32[512,768]{1,0:T(8,128)}) custom-call(s32[9]{0:T(128)} %pad_add_fusion.2.info_ref, f32[8,768]{1,0:T(8,128)} %convert_element_type.342.rest_0_.rest_9_, ...), custom_call_target="tpu_custom_call" | custom-call | flops 4499999744 | bytes 4500000 | tf_op jit(solution)/shard_map/feed_forward/pallas_call | solution.py:337
  106.1 10.4 %feed_forward.3 = (bf16[3072,512]{1,0:T(8,128)(2,1)}, bf16[512,3072]{1,0:T(8,128)(2,1)}, bf16[512,768]{1,0:T(8,128)(2,1)}, f32[512,768]{1,0:T(8,128)}, bf16[512,768]{1,0:T(8,128)(2,1)}, /*index=5*/f32[8,768]{1,0:T(8,128)}) custom-call(s32[5]{0:T(128)} %pad_add_fusion.1.info_ref, ...), custom_call_target="tpu_custom_call", output_to_operand_aliasing={{0}: (10, {}), {1}: (11, {})} | custom-call | flops 1500000000 | bytes 1500000 | tf_op jit(solution)/shard_map/feed_forward/pallas_call | solution.py:337
  117.1 13.8 %feed_back.1 = (bf16[2,4,96,1536]{3,2,1,0:T(8,128)(2,1)}, bf16[2,4,96,1536]{3,2,1,0:T(8,128)(2,1)}, f32[4,1,384]{2,1,0:T(1,128)}, f32[512,768]{1,0:T(8,128)}) custom-call(s32[3]{0:T(128)} %pad_add_fusion.info_ref, bf16[512,768]{1,0:T(8,128)(2,1)} %get-tuple-element.140.grad_outer_ref, bf16[512,768]{1,0:T(8,128)(2,1)} %get-tuple-element.132.rest_7_.normed_low_ref, ...), custom_call_target="tpu_custom_call" | custom-call | flops 3000000000 | bytes 3000000 | tf_op jit(solution)/shard_map/feed_back/pallas_call | solution.py:466
  132.3 3.0 maximum_select_fusion
  135.3 6.7 %project.1 = (bf16[1,768,512]{2,1,0:T(8,128)(2,1)}, bf16[1,768,512]{2,1,0:T(8,128)(2,1)}, bf16[1,768,512]{2,1,0:T(8,128)(2,1)}) custom-call(s32[1]{0:T(128)} %bitcast.2.place_ref, bf16[2048,768]{1,0:T(8,128)(2,1)} %tokens_ref.7, bf16[192,2304]{1,0:T(8,128)(2,1)} %copy-done.3, bf16[3,192,2304]{2,1,0:T(8,128)(2,1)} %bitcast.147, ...), custom_call_target="tpu_custom_call" | custom-call | flops 1250000000 | bytes 1250000 | tf_op jit(solution)/shard_map/project/pallas_call | solution.py:553
  142.0 16.9 %feed_back_own.1 = (bf16[2,4,96,768]{3,2,1,0:T(8,128)(2,1)}, bf16[2,4,96,768]{3,2,1,0:T(8,128)(2,1)}, bf16[2,4,96,768]{3,2,1,0:T(8,128)(2,1)}, bf16[2,4,96,768]{...) custom-call(s32[3]{0:T(128)} %pad_add_fusion.info_ref, ...), custom_call_target="tpu_custom_call" | custom-call | flops 3000000000 | bytes 3000000 | tf_op jit(solution)/shard_map/feed_back_own/pallas_call | solution.py:466
  161.5 22.3 %attend_back.1 = (bf16[3,1,768,512]{3,2,1,0:T(8,128)(2,1)}, bf16[512,768]{1,0:T(8,128)(2,1)}, f32[1,8,768]{2,1,0:T(8,128)}) custom-call(s32[1]{0:T(128)} %bitcast.2.place_ref, s32[4,8]{1,0:T(4,128)} %lengths_ref.3, bf16[512,768]{1,0:T(8,128)(2,1)} %get-tuple-element.155.grad_attended_ref, f32[512,768]{1,0:T(8,128)} %get-tuple-element.156.grad_first_ref, ...), custom_call_target="tpu_custom_call" | custom-call | flops 5000000000 | bytes 5000000 | tf_op jit(solution)/shard_map/attend_back/pallas_call | solution.py:652
  184.0 2.4 collective-permute-done.21
  191.1 5.9 %attention_grads.2 = (bf16[4,2,48,768]{3,2,1,0:T(8,128)(2,1)}, bf16[4,2,48,768]{3,2,1,0:T(8,128)(2,1)}, bf16[4,2,48,768]{3,2,1,0:T(8,128)(2,1)}, bf16[4,2,48,768]{3,2,1,0:T(8,128)(2,1)}) custom-call(s32[4]{0:T(128)} %add_add_fusion.1.info_ref, bf16[3,1,768,512]{3,2,1,0:T(8,128)(2,1)} %get-tuple-element.164.grads_ref, bf16[4,1,208,512]{3,2,1,0:T(8,128)(2,1)} %copy-done.2, ...), custom_call_target="tpu_custom_call" | custom-call | flops 125000000 | bytes 125000 | tf_op jit(solution)/shard_map/attention_grads/pallas_call | solution.py:760
  197.0 4.1 %collective-permute-done.24 = bf16[4,96,768]{2,1,0:T(8,128)(2,1)} collective-permute-done((bf16[4,96,768]{2,1,0:T(8,128)(2,1)S(1)}, bf16[4,96,768]{2,1,0:T(8,128)(2,1)}, u32[]{:S(2)}, u32[]{:S(2)}) %collective-permute-start.24) | collective-permute-done | bytes 589856 | tf_op jit(solution)/shard_map/ppermute | solution.py:799
  201.1 3.0 collective-permute-done.23
  206.4 2.8 collective-permute-start.29
  213.9 2.0 collective-permute-start.37
  220.0 6.6 %attention_grads.3 = (bf16[400,768]{1,0:T(8,128)(2,1)}, bf16[400,768]{1,0:T(8,128)(2,1)}, bf16[400,768]{1,0:T(8,128)(2,1)}, bf16[400,768]{1,0:T(8,128)(2,1)}) custom-call(s32[4]{0:T(128)} %add_add_fusion.info_ref, bf16[3,1,768,512]{3,2,1,0:T(8,128)(2,1)} %get-tuple-element.164.grads_ref, bf16[4,1,208,512]{3,2,1,0:T(8,128)(2,1)} %copy-done.2, ...), custom_call_target="tpu_custom_call" | custom-call | flops 125000000 | bytes 125000 | tf_op jit(solution)/shard_map/attention_grads/pallas_call | solution.py:760
  228.6 11.3 %collective-permute-done.36 = bf16[96,1536]{1,0:T(8,128)(2,1)S(1)} collective-permute-done((bf16[96,1536]{1,0:T(8,128)(2,1)S(1)}, bf16[96,1536]{1,0:T(8,128)(2,1)S(1)}, u32[]{:S(2)}, u32[]{:S(2)}) %collective-permute-start.36) | collective-permute-done | bytes 294944 | tf_op jit(solution)/shard_map/ppermute | solution.py:803
  239.9 2.9 collective-permute-start.32
  242.8 4.2 %copied.2 = bf16[2048,768]{1,0:T(8,128)(2,1)} custom-call(bf16[2048,768]{1,0:T(8,128)(2,1)} %all-gather.5.cloned.1.call-done.from_ref), custom_call_target="tpu_custom_call" | custom-call | flops 125000000 | bytes 125000 | tf_op jit(solution)/shard_map/copied/pallas_call | solution.py:522
  247.0 3.2 %collective-permute-done.37 = bf16[96,1536]{1,0:T(8,128)(2,1)S(1)} collective-permute-done((bf16[96,1536]{1,0:T(8,128)(2,1)S(1)}, bf16[96,1536]{1,0:T(8,128)(2,1)S(1)}, u32[]{:S(2)}, u32[]{:S(2)}) %collective-permute-start.37) | collective-permute-done | bytes 294944 | tf_op jit(solution)/shard_map/ppermute | solution.py:803
  250.2 17.4 %collective-permute-done.38 = bf16[96,1536]{1,0:T(8,128)(2,1)S(1)} collective-permute-done((bf16[96,1536]{1,0:T(8,128)(2,1)S(1)}, bf16[96,1536]{1,0:T(8,128)(2,1)S(1)}, u32[]{:S(2)}, u32[]{:S(2)}) %collective-permute-start.38) | collective-permute-done | bytes 294944 | tf_op jit(solution)/shard_map/ppermute | solution.py:803
  271.6 2.2 collective-permute-start.33
  273.8 2.2 collective-permute-start.34
  277.9 4.2 %copied.3 = bf16[2048,768]{1,0:T(8,128)(2,1)} custom-call(bf16[2048,768]{1,0:T(8,128)(2,1)} %all-gather.7.cloned.1.call-done.from_ref), custom_call_target="tpu_custom_call" | custom-call | flops 125000000 | bytes 125000 | tf_op jit(solution)/shard_map/copied/pallas_call | solution.py:522
  283.6 4.1 %collective-permute-done.34 = bf16[112,768]{1,0:T(8,128)(2,1)S(1)} collective-permute-done((bf16[112,768]{1,0:T(8,128)(2,1)}, bf16[112,768]{1,0:T(8,128)(2,1)S(1)}, u32[]{:S(2)}, u32[]{:S(2)}) %collective-permute-start.34) | collective-permute-done | bytes 172064 | tf_op jit(solution)/shard_map/ppermute | solution.py:803
  287.6 2.7 collective-permute-done.35
  297.9 4.7 %finish_feed.1 = (f32[768,768]{1,0:T(8,128)}, f32[768,768]{1,0:T(8,128)}) custom-call(s32[1]{0:T(128)} %bitcast.4.core_ref, bf16[4,96,1536]{2,1,0:T(8,128)(2,1)} %bitcast.160, bf16[4,96,1536]{2,1,0:T(8,128)(2,1)} %collective-permute-done.45.other_ref), custom_call_target="tpu_custom_call" | custom-call | flops 1250000000 | bytes 1250000 | tf_op jit(solution)/shard_map/finish_feed/pallas_call | solution.py:497
  (246 shorter events, 80.1 us)
Async XLA Ops:
  7.2 72.3 %all-gather.9.cloned.1.call-start = ((), (), s32[]{:S(2)}) async-start(), calls=%async_computation.3 | async-start | bytes 1216512 | tf_op jit(solution)/shard_map/all_gather | solution.py:807
  9.9 17.1 %collective-permute-start = (bf16[96,1536]{1,0:T(8,128)(2,1)S(1)}, bf16[96,1536]{1,0:T(8,128)(2,1)S(1)}, u32[]{:S(2)}, u32[]{:S(2)}) collective-permute-start(bf16[96,1536]{1,0:T(8,128)(2,1)S(1)} %pad_maximum_fusion.7), channel_id=1, source_target_pairs={{0,1},{1,2},{2,3},{3,0},{4,5},{5,6},{6,7},{7,4},{8,9},{9,10},{10,1... | collective-permute-start | bytes 884744 | tf_op jit(solution)/shard_map/ppermute | solution.py:803
  11.2 25.4 %collective-permute-start.1 = (bf16[96,1536]{1,0:T(8,128)(2,1)S(1)}, bf16[96,1536]{1,0:T(8,128)(2,1)S(1)}, u32[]{:S(2)}, u32[]{:S(2)}) collective-permute-start(bf16[96,1536]{1,0:T(8,128)(2,1)S(1)} %pad_maximum_fusion.7), channel_id=1, source_target_pairs={{0,2},{1,3},{2,0},{3,1},{4,6},{5,7},{6,4},{7,5},{8,10},{9,11},{10,... | collective-permute-start | bytes 884744 | tf_op jit(solution)/shard_map/ppermute | solution.py:803
  12.3 27.2 %collective-permute-start.2 = (bf16[96,1536]{1,0:T(8,128)(2,1)S(1)}, bf16[96,1536]{1,0:T(8,128)(2,1)S(1)}, u32[]{:S(2)}, u32[]{:S(2)}) collective-permute-start(bf16[96,1536]{1,0:T(8,128)(2,1)S(1)} %pad_maximum_fusion.7), channel_id=1, source_target_pairs={{0,3},{1,0},{2,1},{3,2},{4,7},{5,4},{6,5},{7,6},{8,11},{9,8},{10,9... | collective-permute-start | bytes 884744 | tf_op jit(solution)/shard_map/ppermute | solution.py:803
  40.6 30.8 %all-to-all-start = ((bf16[4,1,208,512]{3,2,1,0:T(8,128)(2,1)}), bf16[4,1,208,512]{3,2,1,0:T(8,128)(2,1)S(1)}, u32[]{:S(2)}, u32[]{:S(2)}) async-start(bf16[4,1,208,512]{3,2,1,0:T(8,128)(2,1)} %attend_forward.1), calls=%async_computation | async-start | bytes 1703936 | tf_op jit(solution)/shard_map/all_to_all | solution.py:912
  44.2 142.3 %all-gather.5.cloned.1.call-start = ((), (), s32[]{:S(2)}) async-start(), calls=%async_computation.1 | async-start | bytes 3932160 | tf_op jit(solution)/shard_map/all_gather | solution.py:964
  44.2 22.2 %collective-permute-start.3 = (bf16[3,96,1536]{2,1,0:T(8,128)(2,1)}, bf16[3,96,1536]{2,1,0:T(8,128)(2,1)}, u32[]{:S(2)}, u32[]{:S(2)}) collective-permute-start(bf16[3,96,1536]{2,1,0:T(8,128)(2,1)} %pad_maximum_fusion.3.rest_3_.rest_0_), channel_id=1, source_target_pairs={{0,8},{4,12},{8,0},{12,4},{16,24},{20,28},{24,16},{28,20},{1,9},{5... | collective-permute-start | bytes 2654216 | tf_op jit(solution)/shard_map/ppermute | solution.py:799
  45.5 23.3 %collective-permute-start.4 = (bf16[3,96,1536]{2,1,0:T(8,128)(2,1)}, bf16[3,96,1536]{2,1,0:T(8,128)(2,1)}, u32[]{:S(2)}, u32[]{:S(2)}) collective-permute-start(bf16[3,96,1536]{2,1,0:T(8,128)(2,1)} %pad_maximum_fusion.3.rest_3_.rest_0_), channel_id=1, source_target_pairs={{0,16},{4,20},{8,24},{12,28},{16,0},{20,4},{24,8},{28,12},{1,17},{... | collective-permute-start | bytes 2654216 | tf_op jit(solution)/shard_map/ppermute | solution.py:799
  47.8 24.8 %collective-permute-start.5 = (bf16[24,2304]{1,0:T(8,128)(2,1)S(1)}, bf16[24,2304]{1,0:T(8,128)(2,1)S(1)}, u32[]{:S(2)}, u32[]{:S(2)}) collective-permute-start(bf16[24,2304]{1,0:T(8,128)(2,1)S(1)} %constant_dynamic-slice_fusion.1), channel_id=1, source_target_pairs={{0,1},{1,2},{2,3},{3,0},{4,5},{5,6},{6,7},{7,4},{8,9},{9,10},{10,1... | collective-permute-start | bytes 331784 | tf_op jit(solution)/shard_map/ppermute | solution.py:803
  48.2 27.3 %collective-permute-start.6 = (bf16[24,2304]{1,0:T(8,128)(2,1)S(1)}, bf16[24,2304]{1,0:T(8,128)(2,1)S(1)}, u32[]{:S(2)}, u32[]{:S(2)}) collective-permute-start(bf16[24,2304]{1,0:T(8,128)(2,1)S(1)} %constant_dynamic-slice_fusion.1), channel_id=1, source_target_pairs={{0,2},{1,3},{2,0},{3,1},{4,6},{5,7},{6,4},{7,5},{8,10},{9,11},{10,... | collective-permute-start | bytes 331784 | tf_op jit(solution)/shard_map/ppermute | solution.py:803
  49.2 28.1 %collective-permute-start.7 = (bf16[24,2304]{1,0:T(8,128)(2,1)S(1)}, bf16[24,2304]{1,0:T(8,128)(2,1)S(1)}, u32[]{:S(2)}, u32[]{:S(2)}) collective-permute-start(bf16[24,2304]{1,0:T(8,128)(2,1)S(1)} %constant_dynamic-slice_fusion.1), channel_id=1, source_target_pairs={{0,3},{1,0},{2,1},{3,2},{4,7},{5,4},{6,5},{7,6},{8,11},{9,8},{10,9... | collective-permute-start | bytes 331784 | tf_op jit(solution)/shard_map/ppermute | solution.py:803
  67.4 35.1 %collective-permute-start.11 = (bf16[3,48,1536]{2,1,0:T(8,128)(2,1)S(1)}, bf16[3,48,1536]{2,1,0:T(8,128)(2,1)S(1)}, u32[]{:S(2)}, u32[]{:S(2)}) collective-permute-start(bf16[3,48,1536]{2,1,0:T(8,128)(2,1)S(1)} %slice.349), channel_id=1, source_target_pairs={{0,16},{4,20},{8,24},{12,28},{16,0},{20,4},{24,8},{28,12},{1,17},{... | collective-permute-start | bytes 1327112 | tf_op jit(solution)/shard_map/ppermute | solution.py:799
  70.6 31.9 %collective-permute-start.12 = (bf16[3,48,1536]{2,1,0:T(8,128)(2,1)}, bf16[3,48,1536]{2,1,0:T(8,128)(2,1)S(1)}, u32[]{:S(2)}, u32[]{:S(2)}) collective-permute-start(bf16[3,48,1536]{2,1,0:T(8,128)(2,1)} %slice.350), channel_id=1, source_target_pairs={{0,8},{4,12},{8,0},{12,4},{16,24},{20,28},{24,16},{28,20},{1,9},{5... | collective-permute-start | bytes 1327112 | tf_op jit(solution)/shard_map/ppermute | solution.py:799
  82.2 20.4 %collective-permute-start.13 = (bf16[3,24,2304]{2,1,0:T(8,128)(2,1)S(1)}, bf16[3,24,2304]{2,1,0:T(8,128)(2,1)S(1)}, u32[]{:S(2)}, u32[]{:S(2)}) collective-permute-start(bf16[3,24,2304]{2,1,0:T(8,128)(2,1)S(1)} %get-tuple-element.237), channel_id=1, source_target_pairs={{0,8},{4,12},{8,0},{12,4},{16,24},{20,28},{24,16},{28,20},{1,9},{5... | collective-permute-start | bytes 995336 | tf_op jit(solution)/shard_map/ppermute | solution.py:799
  83.6 19.0 %collective-permute-start.14 = (bf16[3,24,2304]{2,1,0:T(8,128)(2,1)S(1)}, bf16[3,24,2304]{2,1,0:T(8,128)(2,1)S(1)}, u32[]{:S(2)}, u32[]{:S(2)}) collective-permute-start(bf16[3,24,2304]{2,1,0:T(8,128)(2,1)S(1)} %get-tuple-element.237), channel_id=1, source_target_pairs={{0,16},{4,20},{8,24},{12,28},{16,0},{20,4},{24,8},{28,12},{1,17},{... | collective-permute-start | bytes 995336 | tf_op jit(solution)/shard_map/ppermute | solution.py:799
  84.8 17.7 %collective-permute-start.15 = (bf16[3,24,2304]{2,1,0:T(8,128)(2,1)S(1)}, bf16[3,24,2304]{2,1,0:T(8,128)(2,1)S(1)}, u32[]{:S(2)}, u32[]{:S(2)}) collective-permute-start(bf16[3,24,2304]{2,1,0:T(8,128)(2,1)S(1)} %get-tuple-element.237), channel_id=1, source_target_pairs={{0,24},{4,28},{8,16},{12,20},{16,8},{20,12},{24,0},{28,4},{1,25},{... | collective-permute-start | bytes 995336 | tf_op jit(solution)/shard_map/ppermute | solution.py:799
  104.0 13.1 %collective-permute-start.18 = (bf16[4,3,24,2304]{3,2,0,1:T(8,128)(2,1)S(1)}, bf16[4,3,24,2304]{3,2,0,1:T(8,128)(2,1)}, u32[]{:S(2)}, u32[]{:S(2)}) collective-permute-start(bf16[4,3,24,2304]{3,2,0,1:T(8,128)(2,1)S(1)} %bitcast.151), channel_id=1, source_target_pairs={{0,4},{4,0},{8,12},{12,8},{16,20},{20,16},{24,28},{28,24},{1,5},{5... | collective-permute-start | bytes 3981320 | tf_op jit(solution)/shard_map/ppermute | solution.py:799
  116.5 161.4 %all-gather.7.cloned.1.call-start = ((), (), s32[]{:S(2)}) async-start(), calls=%async_computation.2 | async-start | bytes 3932160 | tf_op jit(solution)/shard_map/all_gather | solution.py:1009
  158.9 27.5 %collective-permute-start.21 = (bf16[2,4,96,768]{3,2,1,0:T(8,128)(2,1)}, bf16[2,4,96,768]{3,2,1,0:T(8,128)(2,1)}, u32[]{:S(2)}, u32[]{:S(2)}) collective-permute-start(bf16[2,4,96,768]{3,2,1,0:T(8,128)(2,1)} %get-tuple-element.161), channel_id=1, source_target_pairs={{0,16},{4,20},{8,24},{12,28},{16,0},{20,4},{24,8},{28,12},{1,17},{... | collective-permute-start | bytes 3538952 | tf_op jit(solution)/shard_map/ppermute | solution.py:799
  159.3 27.1 %collective-permute-start.22 = (bf16[2,4,96,768]{3,2,1,0:T(8,128)(2,1)}, bf16[2,4,96,768]{3,2,1,0:T(8,128)(2,1)}, u32[]{:S(2)}, u32[]{:S(2)}) collective-permute-start(bf16[2,4,96,768]{3,2,1,0:T(8,128)(2,1)} %get-tuple-element.162), channel_id=1, source_target_pairs={{0,8},{4,12},{8,0},{12,4},{16,24},{20,28},{24,16},{28,20},{1,9},{5... | collective-permute-start | bytes 3538952 | tf_op jit(solution)/shard_map/ppermute | solution.py:799
  187.7 13.4 %collective-permute-start.24 = (bf16[4,96,768]{2,1,0:T(8,128)(2,1)S(1)}, bf16[4,96,768]{2,1,0:T(8,128)(2,1)}, u32[]{:S(2)}, u32[]{:S(2)}) collective-permute-start(bf16[4,96,768]{2,1,0:T(8,128)(2,1)S(1)} %fusion.5), channel_id=1, source_target_pairs={{0,16},{4,20},{8,24},{12,28},{16,0},{20,4},{24,8},{28,12},{1,17},{... | collective-permute-start | bytes 1769480 | tf_op jit(solution)/shard_map/ppermute | solution.py:799
  190.8 13.3 %collective-permute-start.23 = (bf16[4,96,768]{2,1,0:T(8,128)(2,1)}, bf16[4,96,768]{2,1,0:T(8,128)(2,1)}, u32[]{:S(2)}, u32[]{:S(2)}) collective-permute-start(bf16[4,96,768]{2,1,0:T(8,128)(2,1)} %fusion.4), channel_id=1, source_target_pairs={{0,8},{4,12},{8,0},{12,4},{16,24},{20,28},{24,16},{28,20},{1,9},{5... | collective-permute-start | bytes 1769480 | tf_op jit(solution)/shard_map/ppermute | solution.py:799
  213.4 26.4 %collective-permute-start.36 = (bf16[96,1536]{1,0:T(8,128)(2,1)S(1)}, bf16[96,1536]{1,0:T(8,128)(2,1)S(1)}, u32[]{:S(2)}, u32[]{:S(2)}) collective-permute-start(bf16[96,1536]{1,0:T(8,128)(2,1)S(1)} %pad_maximum_fusion.8), channel_id=1, source_target_pairs={{0,3},{1,0},{2,1},{3,2},{4,7},{5,4},{6,5},{7,6},{8,11},{9,8},{10,9... | collective-permute-start | bytes 884744 | tf_op jit(solution)/shard_map/ppermute | solution.py:803
  213.9 36.3 %collective-permute-start.37 = (bf16[96,1536]{1,0:T(8,128)(2,1)S(1)}, bf16[96,1536]{1,0:T(8,128)(2,1)S(1)}, u32[]{:S(2)}, u32[]{:S(2)}) collective-permute-start(bf16[96,1536]{1,0:T(8,128)(2,1)S(1)} %pad_maximum_fusion.9), channel_id=1, source_target_pairs={{0,2},{1,3},{2,0},{3,1},{4,6},{5,7},{6,4},{7,5},{8,10},{9,11},{10,... | collective-permute-start | bytes 884744 | tf_op jit(solution)/shard_map/ppermute | solution.py:803
  215.9 51.7 %collective-permute-start.38 = (bf16[96,1536]{1,0:T(8,128)(2,1)S(1)}, bf16[96,1536]{1,0:T(8,128)(2,1)S(1)}, u32[]{:S(2)}, u32[]{:S(2)}) collective-permute-start(bf16[96,1536]{1,0:T(8,128)(2,1)S(1)} %pad_maximum_fusion.10), channel_id=1, source_target_pairs={{0,1},{1,2},{2,3},{3,0},{4,5},{5,6},{6,7},{7,4},{8,9},{9,10},{10,1... | collective-permute-start | bytes 884744 | tf_op jit(solution)/shard_map/ppermute | solution.py:803
  226.6 43.9 %collective-permute-start.30 = (bf16[400,768]{1,0:T(8,128)(2,1)}, bf16[400,768]{1,0:T(8,128)(2,1)S(1)}, u32[]{:S(2)}, u32[]{:S(2)}) collective-permute-start(bf16[400,768]{1,0:T(8,128)(2,1)} %get-tuple-element.186), channel_id=1, source_target_pairs={{0,8},{4,12},{8,0},{12,4},{16,24},{20,28},{24,16},{28,20},{1,9},{5... | collective-permute-start | bytes 1843208 | tf_op jit(solution)/shard_map/ppermute | solution.py:799
  227.5 43.0 %collective-permute-start.31 = (bf16[400,768]{1,0:T(8,128)(2,1)}, bf16[400,768]{1,0:T(8,128)(2,1)S(1)}, u32[]{:S(2)}, u32[]{:S(2)}) collective-permute-start(bf16[400,768]{1,0:T(8,128)(2,1)} %get-tuple-element.187), channel_id=1, source_target_pairs={{0,16},{4,20},{8,24},{12,28},{16,0},{20,4},{24,8},{28,12},{1,17},{... | collective-permute-start | bytes 1843208 | tf_op jit(solution)/shard_map/ppermute | solution.py:799
  239.9 30.7 %collective-permute-start.32 = (bf16[400,768]{1,0:T(8,128)(2,1)}, bf16[400,768]{1,0:T(8,128)(2,1)S(1)}, u32[]{:S(2)}, u32[]{:S(2)}) collective-permute-start(bf16[400,768]{1,0:T(8,128)(2,1)} %get-tuple-element.188), channel_id=1, source_target_pairs={{0,24},{4,28},{8,16},{12,20},{16,8},{20,12},{24,0},{28,4},{1,25},{... | collective-permute-start | bytes 1843208 | tf_op jit(solution)/shard_map/ppermute | solution.py:799
  269.3 12.9 %collective-permute-start.40 = (bf16[96,1536]{1,0:T(8,128)(2,1)S(1)}, bf16[96,1536]{1,0:T(8,128)(2,1)S(1)}, u32[]{:S(2)}, u32[]{:S(2)}) collective-permute-start(bf16[96,1536]{1,0:T(8,128)(2,1)S(1)} %add_convert_fusion.2), channel_id=1, source_target_pairs={{0,16},{4,20},{8,24},{12,28},{16,0},{20,4},{24,8},{28,12},{1,17},{... | collective-permute-start | bytes 884744 | tf_op jit(solution)/shard_map/ppermute | solution.py:799
  270.5 13.1 %collective-permute-start.41 = (bf16[96,1536]{1,0:T(8,128)(2,1)S(1)}, bf16[96,1536]{1,0:T(8,128)(2,1)S(1)}, u32[]{:S(2)}, u32[]{:S(2)}) collective-permute-start(bf16[96,1536]{1,0:T(8,128)(2,1)S(1)} %add_convert_fusion.2), channel_id=1, source_target_pairs={{0,24},{4,28},{8,16},{12,20},{16,8},{20,12},{24,0},{28,4},{1,25},{... | collective-permute-start | bytes 884744 | tf_op jit(solution)/shard_map/ppermute | solution.py:799
  273.8 13.8 %collective-permute-start.34 = (bf16[112,768]{1,0:T(8,128)(2,1)}, bf16[112,768]{1,0:T(8,128)(2,1)S(1)}, u32[]{:S(2)}, u32[]{:S(2)}) collective-permute-start(bf16[112,768]{1,0:T(8,128)(2,1)} %get-tuple-element.239), channel_id=1, source_target_pairs={{0,2},{1,3},{2,0},{3,1},{4,6},{5,7},{6,4},{7,5},{8,10},{9,11},{10,... | collective-permute-start | bytes 516104 | tf_op jit(solution)/shard_map/ppermute | solution.py:803
  276.0 14.3 %collective-permute-start.35 = (bf16[112,768]{1,0:T(8,128)(2,1)}, bf16[112,768]{1,0:T(8,128)(2,1)}, u32[]{:S(2)}, u32[]{:S(2)}) collective-permute-start(bf16[112,768]{1,0:T(8,128)(2,1)} %get-tuple-element.238), channel_id=1, source_target_pairs={{0,3},{1,0},{2,1},{3,2},{4,7},{5,4},{6,5},{7,6},{8,11},{9,8},{10,9... | collective-permute-start | bytes 516104 | tf_op jit(solution)/shard_map/ppermute | solution.py:803
  (53 other events, 342.1 us)
Sparse Core Ops, SparseCore 0:
  14.5 64.9 all-gather.8
  116.6 61.1 all-gather.4
  184.0 85.6 all-gather.6
where the time goes:
time: 316 us; the launch traced here: 315 us
  Pallas kernels  123 us (39%)
  waiting for transfers between devices  82.8 us (26%)
  starting transfers between devices  51.4 us (16%)
  other arithmetic  27.2 us (9%)
  local copies, waits for them, and re-layouts  15.5 us (5%)
  between operations  14.6 us (5%)
    ppermute x12, waiting for transfers between devices, shift(): return lax.ppermute(array, 'tensor', [(i, (i + by) % n) for i in range(n)])  56.9 us
    pallas_call x2, Pallas kernels, feed_back(): pl.pallas_call(functools.partial(feed_back_kernel, keeps), grid_spec=pltp...  30.7 us
    ppermute x35, starting transfers between devices, swap(): return lax.ppermute(array, 'dp', [(i, i ^ bits) for i in range(self.n_dp)])  30.7 us
    pallas_call x2, Pallas kernels, feed_forward(): pl.pallas_call(functools.partial(feed_forward_kernel, chunks, first is no...  26.1 us
    ppermute x35, waiting for transfers between devices, swap(): return lax.ppermute(array, 'dp', [(i, i ^ bits) for i in range(self.n_dp)])  24.3 us
    pallas_call x1, Pallas kernels, attend_back(): pl.pallas_call(attend_back_kernel, grid_spec=pltpu.PrefetchScalarGridSpec...  22.3 us
    ppermute x12, starting transfers between devices, shift(): return lax.ppermute(array, 'tensor', [(i, (i + by) % n) for i in range(n)])  17.2 us
    pallas_call x2, Pallas kernels, attention_grads(): pl.pallas_call(functools.partial(attention_grads_kernel, n_places, other...  12.5 us
  transfers between devices with their start and end apart: 51, of which 23 were waited for; matrix products, arithmetic and copies ran while one was open for 11% of the time, Pallas kernels for 39%

commit v1 on v0

--- a/solution.py
+++ b/solution.py
@@ -890,11 +890,11 @@
         ],
         axis=1,
     )
+    mixer_piece = lax.dynamic_slice_in_dim(output_weight, index * head_rows, head_rows, 0)
+    piece, mixer_piece = together(piece, mixer_piece)
     line = [plane.shift(piece, s) for s in others]
 
-    mixer = plane.gather(
-        lax.dynamic_slice_in_dim(output_weight, index * head_rows, head_rows, 0)
-    ).reshape(width, width)
+    mixer = plane.gather(mixer_piece).reshape(width, width)
     query_t, key_t, value_t = query_weight.T, key_weight.T, value_weight.T
 
     key_mask_rows = key_mask.reshape(all_blocks, 1, BUCKET)

time: 316 us -> 317 us (level)
  transfers between devices with their start and end apart: 51 -> 51, of which waited for: 23 -> 24; matrix products, arithmetic and copies ran while one was open for 11% -> 11% of each run, Pallas kernels for 39% -> 39%
where the time goes in v1:
time: 317 us; the launch traced here: 315 us
  Pallas kernels  123 us (39%)
  waiting for transfers between devices  83.2 us (26%)
  starting transfers between devices  51.6 us (16%)
  other arithmetic  27.2 us (9%)
  local copies, waits for them, and re-layouts  15.5 us (5%)
  between operations  14.6 us (5%)
    ppermute x12, waiting for transfers between devices, shift(): return lax.ppermute(array, 'tensor', [(i, (i + by) % n) for i in range(n)])  57.4 us
    ppermute x35, starting transfers between devices, swap(): return lax.ppermute(array, 'dp', [(i, i ^ bits) for i in range(self.n_dp)])  31 us
    pallas_call x2, Pallas kernels, feed_back(): pl.pallas_call(functools.partial(feed_back_kernel, keeps), grid_spec=pltp...  30.6 us
    pallas_call x2, Pallas kernels, feed_forward(): pl.pallas_call(functools.partial(feed_forward_kernel, chunks, first is no...  26.1 us
    ppermute x35, waiting for transfers between devices, swap(): return lax.ppermute(array, 'dp', [(i, i ^ bits) for i in range(self.n_dp)])  24.2 us
    pallas_call x1, Pallas kernels, attend_back(): pl.pallas_call(attend_back_kernel, grid_spec=pltpu.PrefetchScalarGridSpec...  22.4 us
    ppermute x12, starting transfers between devices, shift(): return lax.ppermute(array, 'tensor', [(i, (i + by) % n) for i in range(n)])  17.1 us
    pallas_call x2, Pallas kernels, attention_grads(): pl.pallas_call(functools.partial(attention_grads_kernel, n_places, other...  12.5 us
  transfers between devices with their start and end apart: 51, of which 24 were waited for; matrix products, arithmetic and copies ran while one was open for 11% of the time, Pallas kernels for 39%

profile of v1, /device:TPU:9, one launch (start us, length us, event | category | flops | bytes accessed | tf_op | source)
XLA Modules:
  0.0 315.2 jit_solution(3911958408511299431)
XLA Ops:
  15.1 11.8 %attend_forward.1 = bf16[4,1,208,512]{3,2,1,0:T(8,128)(2,1)} custom-call(s32[4,8]{1,0:T(4,128)} %lengths_ref.3, bf16[2048,768]{1,0:T(8,128)(2,1)} %tokens_ref.7, bf16[192,768]{1,0:T(8,128)(2,1)} %bitcast.169, bf16[192,768]{1,0:T(8,128)(2,1)} %bitcast.171, bf16[192,768]{1,0:T(8,128)(2,1)} %bitcast.173, bf16[16,512]{1,0:T(8,128)(2,1)} %reshape.149.biases_ref, ...), custom_call_target="tpu_custom_call" | custom-call | flops 3000000000 | bytes 3000000 | tf_op jit(solution)/shard_map/attend_forward/pallas_call | solution.py:121
  26.9 10.3 %collective-permute-done.1 = bf16[96,1536]{1,0:T(8,128)(2,1)S(1)} collective-permute-done((bf16[96,1536]{1,0:T(8,128)(2,1)S(1)}, bf16[96,1536]{1,0:T(8,128)(2,1)S(1)}, u32[]{:S(2)}, u32[]{:S(2)}) %collective-permute-start.1) | collective-permute-done | bytes 294944 | tf_op jit(solution)/shard_map/ppermute | solution.py:803
  37.2 2.9 collective-permute-done.2
  41.2 3.5 %all-to-all-start = ((bf16[4,1,208,512]{3,2,1,0:T(8,128)(2,1)}), bf16[4,1,208,512]{3,2,1,0:T(8,128)(2,1)S(1)}, u32[]{:S(2)}, u32[]{:S(2)}) async-start(bf16[4,1,208,512]{3,2,1,0:T(8,128)(2,1)} %attend_forward.1), calls=%async_computation | async-start | bytes 1703936 | tf_op jit(solution)/shard_map/all_to_all | solution.py:912
  52.6 2.8 pad_maximum_fusion.rest_2_.own_ref
  55.4 11.6 %collective-permute-done.3.rest_4_.rest_1_ = bf16[3,96,1536]{2,1,0:T(8,128)(2,1)} collective-permute-done((bf16[3,96,1536]{2,1,0:T(8,128)(2,1)}, bf16[3,96,1536]{2,1,0:T(8,128)(2,1)}, u32[]{:S(2)}, u32[]{:S(2)}) %collective-permute-start.3) | collective-permute-done | bytes 884768 | tf_op jit(solution)/shard_map/ppermute | solution.py:799
  73.2 2.9 collective-permute-done.6
  87.4 15.7 %feed_forward.2 = (bf16[3072,512]{1,0:T(8,128)(2,1)}, bf16[512,3072]{1,0:T(8,128)(2,1)}, bf16[512,768]{1,0:T(8,128)(2,1)}, f32[512,768]{1,0:T(8,128)}, f32[512,1]{1,0:T(8,128)}, /*index=5*/f32[512,768]{1,0:T(8,128)}) custom-call(s32[9]{0:T(128)} %pad_add_fusion.2.info_ref, f32[8,768]{1,0:T(8,128)} %convert_element_type.342.rest_0_.rest_9_, ...), custom_call_target="tpu_custom_call" | custom-call | flops 4499999744 | bytes 4500000 | tf_op jit(solution)/shard_map/feed_forward/pallas_call | solution.py:337
  106.7 10.4 %feed_forward.3 = (bf16[3072,512]{1,0:T(8,128)(2,1)}, bf16[512,3072]{1,0:T(8,128)(2,1)}, bf16[512,768]{1,0:T(8,128)(2,1)}, f32[512,768]{1,0:T(8,128)}, bf16[512,768]{1,0:T(8,128)(2,1)}, /*index=5*/f32[8,768]{1,0:T(8,128)}) custom-call(s32[5]{0:T(128)} %pad_add_fusion.1.info_ref, ...), custom_call_target="tpu_custom_call", output_to_operand_aliasing={{0}: (10, {}), {1}: (11, {})} | custom-call | flops 1500000000 | bytes 1500000 | tf_op jit(solution)/shard_map/feed_forward/pallas_call | solution.py:337
  117.7 13.8 %feed_back.1 = (bf16[2,4,96,1536]{3,2,1,0:T(8,128)(2,1)}, bf16[2,4,96,1536]{3,2,1,0:T(8,128)(2,1)}, f32[4,1,384]{2,1,0:T(1,128)}, f32[512,768]{1,0:T(8,128)}) custom-call(s32[3]{0:T(128)} %pad_add_fusion.info_ref, bf16[512,768]{1,0:T(8,128)(2,1)} %get-tuple-element.144.grad_outer_ref, bf16[512,768]{1,0:T(8,128)(2,1)} %get-tuple-element.136.rest_7_.normed_low_ref, ...), custom_call_target="tpu_custom_call" | custom-call | flops 3000000000 | bytes 3000000 | tf_op jit(solution)/shard_map/feed_back/pallas_call | solution.py:466
  132.9 3.0 maximum_select_fusion
  135.9 6.7 %project.1 = (bf16[1,768,512]{2,1,0:T(8,128)(2,1)}, bf16[1,768,512]{2,1,0:T(8,128)(2,1)}, bf16[1,768,512]{2,1,0:T(8,128)(2,1)}) custom-call(s32[1]{0:T(128)} %bitcast.2.place_ref, bf16[2048,768]{1,0:T(8,128)(2,1)} %tokens_ref.7, bf16[192,2304]{1,0:T(8,128)(2,1)} %copy-done.3, bf16[3,192,2304]{2,1,0:T(8,128)(2,1)} %bitcast.147, ...), custom_call_target="tpu_custom_call" | custom-call | flops 1250000000 | bytes 1250000 | tf_op jit(solution)/shard_map/project/pallas_call | solution.py:553
  142.6 16.9 %feed_back_own.1 = (bf16[2,4,96,768]{3,2,1,0:T(8,128)(2,1)}, bf16[2,4,96,768]{3,2,1,0:T(8,128)(2,1)}, bf16[2,4,96,768]{3,2,1,0:T(8,128)(2,1)}, bf16[2,4,96,768]{...) custom-call(s32[3]{0:T(128)} %pad_add_fusion.info_ref, ...), custom_call_target="tpu_custom_call" | custom-call | flops 3000000000 | bytes 3000000 | tf_op jit(solution)/shard_map/feed_back_own/pallas_call | solution.py:466
  162.1 22.4 %attend_back.1 = (bf16[3,1,768,512]{3,2,1,0:T(8,128)(2,1)}, bf16[512,768]{1,0:T(8,128)(2,1)}, f32[1,8,768]{2,1,0:T(8,128)}) custom-call(s32[1]{0:T(128)} %bitcast.2.place_ref, s32[4,8]{1,0:T(4,128)} %lengths_ref.3, bf16[512,768]{1,0:T(8,128)(2,1)} %get-tuple-element.159.grad_attended_ref, f32[512,768]{1,0:T(8,128)} %get-tuple-element.160.grad_first_ref, ...), custom_call_target="tpu_custom_call" | custom-call | flops 5000000000 | bytes 5000000 | tf_op jit(solution)/shard_map/attend_back/pallas_call | solution.py:652
  184.6 2.4 collective-permute-done.21
  191.8 5.9 %attention_grads.2 = (bf16[4,2,48,768]{3,2,1,0:T(8,128)(2,1)}, bf16[4,2,48,768]{3,2,1,0:T(8,128)(2,1)}, bf16[4,2,48,768]{3,2,1,0:T(8,128)(2,1)}, bf16[4,2,48,768]{3,2,1,0:T(8,128)(2,1)}) custom-call(s32[4]{0:T(128)} %add_add_fusion.1.info_ref, bf16[3,1,768,512]{3,2,1,0:T(8,128)(2,1)} %get-tuple-element.168.grads_ref, bf16[4,1,208,512]{3,2,1,0:T(8,128)(2,1)} %copy-done.2, ...), custom_call_target="tpu_custom_call" | custom-call | flops 125000000 | bytes 125000 | tf_op jit(solution)/shard_map/attention_grads/pallas_call | solution.py:760
  197.7 4.0 %collective-permute-done.24 = bf16[4,96,768]{2,1,0:T(8,128)(2,1)} collective-permute-done((bf16[4,96,768]{2,1,0:T(8,128)(2,1)S(1)}, bf16[4,96,768]{2,1,0:T(8,128)(2,1)}, u32[]{:S(2)}, u32[]{:S(2)}) %collective-permute-start.24) | collective-permute-done | bytes 589856 | tf_op jit(solution)/shard_map/ppermute | solution.py:799
  201.7 3.0 collective-permute-done.23
  206.9 2.8 collective-permute-start.29
  214.5 2.1 collective-permute-start.37
  220.6 6.6 %attention_grads.3 = (bf16[400,768]{1,0:T(8,128)(2,1)}, bf16[400,768]{1,0:T(8,128)(2,1)}, bf16[400,768]{1,0:T(8,128)(2,1)}, bf16[400,768]{1,0:T(8,128)(2,1)}) custom-call(s32[4]{0:T(128)} %add_add_fusion.info_ref, bf16[3,1,768,512]{3,2,1,0:T(8,128)(2,1)} %get-tuple-element.168.grads_ref, bf16[4,1,208,512]{3,2,1,0:T(8,128)(2,1)} %copy-done.2, ...), custom_call_target="tpu_custom_call" | custom-call | flops 125000000 | bytes 125000 | tf_op jit(solution)/shard_map/attention_grads/pallas_call | solution.py:760
  229.2 11.1 %collective-permute-done.36 = bf16[96,1536]{1,0:T(8,128)(2,1)S(1)} collective-permute-done((bf16[96,1536]{1,0:T(8,128)(2,1)S(1)}, bf16[96,1536]{1,0:T(8,128)(2,1)S(1)}, u32[]{:S(2)}, u32[]{:S(2)}) %collective-permute-start.36) | collective-permute-done | bytes 294944 | tf_op jit(solution)/shard_map/ppermute | solution.py:803
  240.3 3.1 collective-permute-start.32
  243.4 4.2 %copied.2 = bf16[2048,768]{1,0:T(8,128)(2,1)} custom-call(bf16[2048,768]{1,0:T(8,128)(2,1)} %all-gather.5.cloned.1.call-done.from_ref), custom_call_target="tpu_custom_call" | custom-call | flops 125000000 | bytes 125000 | tf_op jit(solution)/shard_map/copied/pallas_call | solution.py:522
  247.6 3.2 %collective-permute-done.37 = bf16[96,1536]{1,0:T(8,128)(2,1)S(1)} collective-permute-done((bf16[96,1536]{1,0:T(8,128)(2,1)S(1)}, bf16[96,1536]{1,0:T(8,128)(2,1)S(1)}, u32[]{:S(2)}, u32[]{:S(2)}) %collective-permute-start.37) | collective-permute-done | bytes 294944 | tf_op jit(solution)/shard_map/ppermute | solution.py:803
  250.8 17.4 %collective-permute-done.38 = bf16[96,1536]{1,0:T(8,128)(2,1)S(1)} collective-permute-done((bf16[96,1536]{1,0:T(8,128)(2,1)S(1)}, bf16[96,1536]{1,0:T(8,128)(2,1)S(1)}, u32[]{:S(2)}, u32[]{:S(2)}) %collective-permute-start.38) | collective-permute-done | bytes 294944 | tf_op jit(solution)/shard_map/ppermute | solution.py:803
  272.2 2.2 collective-permute-start.33
  274.4 2.2 collective-permute-start.34
  278.5 4.2 %copied.3 = bf16[2048,768]{1,0:T(8,128)(2,1)} custom-call(bf16[2048,768]{1,0:T(8,128)(2,1)} %all-gather.7.cloned.1.call-done.from_ref), custom_call_target="tpu_custom_call" | custom-call | flops 125000000 | bytes 125000 | tf_op jit(solution)/shard_map/copied/pallas_call | solution.py:522
  284.1 4.1 %collective-permute-done.34 = bf16[112,768]{1,0:T(8,128)(2,1)S(1)} collective-permute-done((bf16[112,768]{1,0:T(8,128)(2,1)}, bf16[112,768]{1,0:T(8,128)(2,1)S(1)}, u32[]{:S(2)}, u32[]{:S(2)}) %collective-permute-start.34) | collective-permute-done | bytes 172064 | tf_op jit(solution)/shard_map/ppermute | solution.py:803
  288.2 2.7 collective-permute-done.35
  298.4 4.7 %finish_feed.1 = (f32[768,768]{1,0:T(8,128)}, f32[768,768]{1,0:T(8,128)}) custom-call(s32[1]{0:T(128)} %bitcast.4.core_ref, bf16[4,96,1536]{2,1,0:T(8,128)(2,1)} %bitcast.160, bf16[4,96,1536]{2,1,0:T(8,128)(2,1)} %collective-permute-done.45.other_ref), custom_call_target="tpu_custom_call" | custom-call | flops 1250000000 | bytes 1250000 | tf_op jit(solution)/shard_map/finish_feed/pallas_call | solution.py:497
  (246 shorter events, 80.3 us)
Async XLA Ops:
  7.2 72.9 %all-gather.9.cloned.1.call-start = ((), (), s32[]{:S(2)}) async-start(), calls=%async_computation.3 | async-start | bytes 1216512 | tf_op jit(solution)/shard_map/all_gather | solution.py:807
  10.5 16.4 %collective-permute-start = (bf16[96,1536]{1,0:T(8,128)(2,1)S(1)}, bf16[96,1536]{1,0:T(8,128)(2,1)S(1)}, u32[]{:S(2)}, u32[]{:S(2)}) collective-permute-start(bf16[96,1536]{1,0:T(8,128)(2,1)S(1)} %pad_maximum_fusion.7), channel_id=1, source_target_pairs={{0,1},{1,2},{2,3},{3,0},{4,5},{5,6},{6,7},{7,4},{8,9},{9,10},{10,1... | collective-permute-start | bytes 884744 | tf_op jit(solution)/shard_map/ppermute | solution.py:803
  11.8 25.4 %collective-permute-start.1 = (bf16[96,1536]{1,0:T(8,128)(2,1)S(1)}, bf16[96,1536]{1,0:T(8,128)(2,1)S(1)}, u32[]{:S(2)}, u32[]{:S(2)}) collective-permute-start(bf16[96,1536]{1,0:T(8,128)(2,1)S(1)} %pad_maximum_fusion.7), channel_id=1, source_target_pairs={{0,2},{1,3},{2,0},{3,1},{4,6},{5,7},{6,4},{7,5},{8,10},{9,11},{10,... | collective-permute-start | bytes 884744 | tf_op jit(solution)/shard_map/ppermute | solution.py:803
  12.9 27.3 %collective-permute-start.2 = (bf16[96,1536]{1,0:T(8,128)(2,1)S(1)}, bf16[96,1536]{1,0:T(8,128)(2,1)S(1)}, u32[]{:S(2)}, u32[]{:S(2)}) collective-permute-start(bf16[96,1536]{1,0:T(8,128)(2,1)S(1)} %pad_maximum_fusion.7), channel_id=1, source_target_pairs={{0,3},{1,0},{2,1},{3,2},{4,7},{5,4},{6,5},{7,6},{8,11},{9,8},{10,9... | collective-permute-start | bytes 884744 | tf_op jit(solution)/shard_map/ppermute | solution.py:803
  41.2 30.8 %all-to-all-start = ((bf16[4,1,208,512]{3,2,1,0:T(8,128)(2,1)}), bf16[4,1,208,512]{3,2,1,0:T(8,128)(2,1)S(1)}, u32[]{:S(2)}, u32[]{:S(2)}) async-start(bf16[4,1,208,512]{3,2,1,0:T(8,128)(2,1)} %attend_forward.1), calls=%async_computation | async-start | bytes 1703936 | tf_op jit(solution)/shard_map/all_to_all | solution.py:912
  44.7 142.3 %all-gather.5.cloned.1.call-start = ((), (), s32[]{:S(2)}) async-start(), calls=%async_computation.1 | async-start | bytes 3932160 | tf_op jit(solution)/shard_map/all_gather | solution.py:964
  44.8 22.2 %collective-permute-start.3 = (bf16[3,96,1536]{2,1,0:T(8,128)(2,1)}, bf16[3,96,1536]{2,1,0:T(8,128)(2,1)}, u32[]{:S(2)}, u32[]{:S(2)}) collective-permute-start(bf16[3,96,1536]{2,1,0:T(8,128)(2,1)} %pad_maximum_fusion.3.rest_3_.rest_0_), channel_id=1, source_target_pairs={{0,8},{4,12},{8,0},{12,4},{16,24},{20,28},{24,16},{28,20},{1,9},{5... | collective-permute-start | bytes 2654216 | tf_op jit(solution)/shard_map/ppermute | solution.py:799
  46.1 23.3 %collective-permute-start.4 = (bf16[3,96,1536]{2,1,0:T(8,128)(2,1)}, bf16[3,96,1536]{2,1,0:T(8,128)(2,1)}, u32[]{:S(2)}, u32[]{:S(2)}) collective-permute-start(bf16[3,96,1536]{2,1,0:T(8,128)(2,1)} %pad_maximum_fusion.3.rest_3_.rest_0_), channel_id=1, source_target_pairs={{0,16},{4,20},{8,24},{12,28},{16,0},{20,4},{24,8},{28,12},{1,17},{... | collective-permute-start | bytes 2654216 | tf_op jit(solution)/shard_map/ppermute | solution.py:799
  48.4 24.8 %collective-permute-start.5 = (bf16[24,2304]{1,0:T(8,128)(2,1)S(1)}, bf16[24,2304]{1,0:T(8,128)(2,1)S(1)}, u32[]{:S(2)}, u32[]{:S(2)}) collective-permute-start(bf16[24,2304]{1,0:T(8,128)(2,1)S(1)} %constant_dynamic-slice_fusion.1), channel_id=1, source_target_pairs={{0,1},{1,2},{2,3},{3,0},{4,5},{5,6},{6,7},{7,4},{8,9},{9,10},{10,1... | collective-permute-start | bytes 331784 | tf_op jit(solution)/shard_map/ppermute | solution.py:803
  48.8 27.3 %collective-permute-start.6 = (bf16[24,2304]{1,0:T(8,128)(2,1)S(1)}, bf16[24,2304]{1,0:T(8,128)(2,1)S(1)}, u32[]{:S(2)}, u32[]{:S(2)}) collective-permute-start(bf16[24,2304]{1,0:T(8,128)(2,1)S(1)} %constant_dynamic-slice_fusion.1), channel_id=1, source_target_pairs={{0,2},{1,3},{2,0},{3,1},{4,6},{5,7},{6,4},{7,5},{8,10},{9,11},{10,... | collective-permute-start | bytes 331784 | tf_op jit(solution)/shard_map/ppermute | solution.py:803
  49.8 28.2 %collective-permute-start.7 = (bf16[24,2304]{1,0:T(8,128)(2,1)S(1)}, bf16[24,2304]{1,0:T(8,128)(2,1)S(1)}, u32[]{:S(2)}, u32[]{:S(2)}) collective-permute-start(bf16[24,2304]{1,0:T(8,128)(2,1)S(1)} %constant_dynamic-slice_fusion.1), channel_id=1, source_target_pairs={{0,3},{1,0},{2,1},{3,2},{4,7},{5,4},{6,5},{7,6},{8,11},{9,8},{10,9... | collective-permute-start | bytes 331784 | tf_op jit(solution)/shard_map/ppermute | solution.py:803
  68.0 35.1 %collective-permute-start.11 = (bf16[3,48,1536]{2,1,0:T(8,128)(2,1)S(1)}, bf16[3,48,1536]{2,1,0:T(8,128)(2,1)S(1)}, u32[]{:S(2)}, u32[]{:S(2)}) collective-permute-start(bf16[3,48,1536]{2,1,0:T(8,128)(2,1)S(1)} %slice.349), channel_id=1, source_target_pairs={{0,16},{4,20},{8,24},{12,28},{16,0},{20,4},{24,8},{28,12},{1,17},{... | collective-permute-start | bytes 1327112 | tf_op jit(solution)/shard_map/ppermute | solution.py:799
  71.2 31.9 %collective-permute-start.12 = (bf16[3,48,1536]{2,1,0:T(8,128)(2,1)}, bf16[3,48,1536]{2,1,0:T(8,128)(2,1)S(1)}, u32[]{:S(2)}, u32[]{:S(2)}) collective-permute-start(bf16[3,48,1536]{2,1,0:T(8,128)(2,1)} %slice.350), channel_id=1, source_target_pairs={{0,8},{4,12},{8,0},{12,4},{16,24},{20,28},{24,16},{28,20},{1,9},{5... | collective-permute-start | bytes 1327112 | tf_op jit(solution)/shard_map/ppermute | solution.py:799
  82.8 20.4 %collective-permute-start.13 = (bf16[3,24,2304]{2,1,0:T(8,128)(2,1)S(1)}, bf16[3,24,2304]{2,1,0:T(8,128)(2,1)S(1)}, u32[]{:S(2)}, u32[]{:S(2)}) collective-permute-start(bf16[3,24,2304]{2,1,0:T(8,128)(2,1)S(1)} %get-tuple-element.241), channel_id=1, source_target_pairs={{0,8},{4,12},{8,0},{12,4},{16,24},{20,28},{24,16},{28,20},{1,9},{5... | collective-permute-start | bytes 995336 | tf_op jit(solution)/shard_map/ppermute | solution.py:799
  84.2 19.0 %collective-permute-start.14 = (bf16[3,24,2304]{2,1,0:T(8,128)(2,1)S(1)}, bf16[3,24,2304]{2,1,0:T(8,128)(2,1)S(1)}, u32[]{:S(2)}, u32[]{:S(2)}) collective-permute-start(bf16[3,24,2304]{2,1,0:T(8,128)(2,1)S(1)} %get-tuple-element.241), channel_id=1, source_target_pairs={{0,16},{4,20},{8,24},{12,28},{16,0},{20,4},{24,8},{28,12},{1,17},{... | collective-permute-start | bytes 995336 | tf_op jit(solution)/shard_map/ppermute | solution.py:799
  85.4 17.7 %collective-permute-start.15 = (bf16[3,24,2304]{2,1,0:T(8,128)(2,1)S(1)}, bf16[3,24,2304]{2,1,0:T(8,128)(2,1)S(1)}, u32[]{:S(2)}, u32[]{:S(2)}) collective-permute-start(bf16[3,24,2304]{2,1,0:T(8,128)(2,1)S(1)} %get-tuple-element.241), channel_id=1, source_target_pairs={{0,24},{4,28},{8,16},{12,20},{16,8},{20,12},{24,0},{28,4},{1,25},{... | collective-permute-start | bytes 995336 | tf_op jit(solution)/shard_map/ppermute | solution.py:799
  104.6 13.1 %collective-permute-start.18 = (bf16[4,3,24,2304]{3,2,0,1:T(8,128)(2,1)S(1)}, bf16[4,3,24,2304]{3,2,0,1:T(8,128)(2,1)}, u32[]{:S(2)}, u32[]{:S(2)}) collective-permute-start(bf16[4,3,24,2304]{3,2,0,1:T(8,128)(2,1)S(1)} %bitcast.151), channel_id=1, source_target_pairs={{0,4},{4,0},{8,12},{12,8},{16,20},{20,16},{24,28},{28,24},{1,5},{5... | collective-permute-start | bytes 3981320 | tf_op jit(solution)/shard_map/ppermute | solution.py:799
  117.1 161.4 %all-gather.7.cloned.1.call-start = ((), (), s32[]{:S(2)}) async-start(), calls=%async_computation.2 | async-start | bytes 3932160 | tf_op jit(solution)/shard_map/all_gather | solution.py:1009
  159.5 27.5 %collective-permute-start.21 = (bf16[2,4,96,768]{3,2,1,0:T(8,128)(2,1)}, bf16[2,4,96,768]{3,2,1,0:T(8,128)(2,1)}, u32[]{:S(2)}, u32[]{:S(2)}) collective-permute-start(bf16[2,4,96,768]{3,2,1,0:T(8,128)(2,1)} %get-tuple-element.165), channel_id=1, source_target_pairs={{0,16},{4,20},{8,24},{12,28},{16,0},{20,4},{24,8},{28,12},{1,17},{... | collective-permute-start | bytes 3538952 | tf_op jit(solution)/shard_map/ppermute | solution.py:799
  159.9 27.1 %collective-permute-start.22 = (bf16[2,4,96,768]{3,2,1,0:T(8,128)(2,1)}, bf16[2,4,96,768]{3,2,1,0:T(8,128)(2,1)}, u32[]{:S(2)}, u32[]{:S(2)}) collective-permute-start(bf16[2,4,96,768]{3,2,1,0:T(8,128)(2,1)} %get-tuple-element.166), channel_id=1, source_target_pairs={{0,8},{4,12},{8,0},{12,4},{16,24},{20,28},{24,16},{28,20},{1,9},{5... | collective-permute-start | bytes 3538952 | tf_op jit(solution)/shard_map/ppermute | solution.py:799
  188.2 13.4 %collective-permute-start.24 = (bf16[4,96,768]{2,1,0:T(8,128)(2,1)S(1)}, bf16[4,96,768]{2,1,0:T(8,128)(2,1)}, u32[]{:S(2)}, u32[]{:S(2)}) collective-permute-start(bf16[4,96,768]{2,1,0:T(8,128)(2,1)S(1)} %fusion.5), channel_id=1, source_target_pairs={{0,16},{4,20},{8,24},{12,28},{16,0},{20,4},{24,8},{28,12},{1,17},{... | collective-permute-start | bytes 1769480 | tf_op jit(solution)/shard_map/ppermute | solution.py:799
  191.4 13.3 %collective-permute-start.23 = (bf16[4,96,768]{2,1,0:T(8,128)(2,1)}, bf16[4,96,768]{2,1,0:T(8,128)(2,1)}, u32[]{:S(2)}, u32[]{:S(2)}) collective-permute-start(bf16[4,96,768]{2,1,0:T(8,128)(2,1)} %fusion.4), channel_id=1, source_target_pairs={{0,8},{4,12},{8,0},{12,4},{16,24},{20,28},{24,16},{28,20},{1,9},{5... | collective-permute-start | bytes 1769480 | tf_op jit(solution)/shard_map/ppermute | solution.py:799
  214.0 26.3 %collective-permute-start.36 = (bf16[96,1536]{1,0:T(8,128)(2,1)S(1)}, bf16[96,1536]{1,0:T(8,128)(2,1)S(1)}, u32[]{:S(2)}, u32[]{:S(2)}) collective-permute-start(bf16[96,1536]{1,0:T(8,128)(2,1)S(1)} %pad_maximum_fusion.8), channel_id=1, source_target_pairs={{0,3},{1,0},{2,1},{3,2},{4,7},{5,4},{6,5},{7,6},{8,11},{9,8},{10,9... | collective-permute-start | bytes 884744 | tf_op jit(solution)/shard_map/ppermute | solution.py:803
  214.5 36.4 %collective-permute-start.37 = (bf16[96,1536]{1,0:T(8,128)(2,1)S(1)}, bf16[96,1536]{1,0:T(8,128)(2,1)S(1)}, u32[]{:S(2)}, u32[]{:S(2)}) collective-permute-start(bf16[96,1536]{1,0:T(8,128)(2,1)S(1)} %pad_maximum_fusion.9), channel_id=1, source_target_pairs={{0,2},{1,3},{2,0},{3,1},{4,6},{5,7},{6,4},{7,5},{8,10},{9,11},{10,... | collective-permute-start | bytes 884744 | tf_op jit(solution)/shard_map/ppermute | solution.py:803
  216.5 51.7 %collective-permute-start.38 = (bf16[96,1536]{1,0:T(8,128)(2,1)S(1)}, bf16[96,1536]{1,0:T(8,128)(2,1)S(1)}, u32[]{:S(2)}, u32[]{:S(2)}) collective-permute-start(bf16[96,1536]{1,0:T(8,128)(2,1)S(1)} %pad_maximum_fusion.10), channel_id=1, source_target_pairs={{0,1},{1,2},{2,3},{3,0},{4,5},{5,6},{6,7},{7,4},{8,9},{9,10},{10,1... | collective-permute-start | bytes 884744 | tf_op jit(solution)/shard_map/ppermute | solution.py:803
  227.2 43.9 %collective-permute-start.30 = (bf16[400,768]{1,0:T(8,128)(2,1)}, bf16[400,768]{1,0:T(8,128)(2,1)S(1)}, u32[]{:S(2)}, u32[]{:S(2)}) collective-permute-start(bf16[400,768]{1,0:T(8,128)(2,1)} %get-tuple-element.190), channel_id=1, source_target_pairs={{0,8},{4,12},{8,0},{12,4},{16,24},{20,28},{24,16},{28,20},{1,9},{5... | collective-permute-start | bytes 1843208 | tf_op jit(solution)/shard_map/ppermute | solution.py:799
  228.1 43.0 %collective-permute-start.31 = (bf16[400,768]{1,0:T(8,128)(2,1)}, bf16[400,768]{1,0:T(8,128)(2,1)S(1)}, u32[]{:S(2)}, u32[]{:S(2)}) collective-permute-start(bf16[400,768]{1,0:T(8,128)(2,1)} %get-tuple-element.191), channel_id=1, source_target_pairs={{0,16},{4,20},{8,24},{12,28},{16,0},{20,4},{24,8},{28,12},{1,17},{... | collective-permute-start | bytes 1843208 | tf_op jit(solution)/shard_map/ppermute | solution.py:799
  240.3 30.8 %collective-permute-start.32 = (bf16[400,768]{1,0:T(8,128)(2,1)}, bf16[400,768]{1,0:T(8,128)(2,1)S(1)}, u32[]{:S(2)}, u32[]{:S(2)}) collective-permute-start(bf16[400,768]{1,0:T(8,128)(2,1)} %get-tuple-element.192), channel_id=1, source_target_pairs={{0,24},{4,28},{8,16},{12,20},{16,8},{20,12},{24,0},{28,4},{1,25},{... | collective-permute-start | bytes 1843208 | tf_op jit(solution)/shard_map/ppermute | solution.py:799
  269.9 12.8 %collective-permute-start.40 = (bf16[96,1536]{1,0:T(8,128)(2,1)S(1)}, bf16[96,1536]{1,0:T(8,128)(2,1)S(1)}, u32[]{:S(2)}, u32[]{:S(2)}) collective-permute-start(bf16[96,1536]{1,0:T(8,128)(2,1)S(1)} %add_convert_fusion.2), channel_id=1, source_target_pairs={{0,16},{4,20},{8,24},{12,28},{16,0},{20,4},{24,8},{28,12},{1,17},{... | collective-permute-start | bytes 884744 | tf_op jit(solution)/shard_map/ppermute | solution.py:799
  271.1 13.1 %collective-permute-start.41 = (bf16[96,1536]{1,0:T(8,128)(2,1)S(1)}, bf16[96,1536]{1,0:T(8,128)(2,1)S(1)}, u32[]{:S(2)}, u32[]{:S(2)}) collective-permute-start(bf16[96,1536]{1,0:T(8,128)(2,1)S(1)} %add_convert_fusion.2), channel_id=1, source_target_pairs={{0,24},{4,28},{8,16},{12,20},{16,8},{20,12},{24,0},{28,4},{1,25},{... | collective-permute-start | bytes 884744 | tf_op jit(solution)/shard_map/ppermute | solution.py:799
  274.4 13.9 %collective-permute-start.34 = (bf16[112,768]{1,0:T(8,128)(2,1)}, bf16[112,768]{1,0:T(8,128)(2,1)S(1)}, u32[]{:S(2)}, u32[]{:S(2)}) collective-permute-start(bf16[112,768]{1,0:T(8,128)(2,1)} %get-tuple-element.243), channel_id=1, source_target_pairs={{0,2},{1,3},{2,0},{3,1},{4,6},{5,7},{6,4},{7,5},{8,10},{9,11},{10,... | collective-permute-start | bytes 516104 | tf_op jit(solution)/shard_map/ppermute | solution.py:803
  276.6 14.3 %collective-permute-start.35 = (bf16[112,768]{1,0:T(8,128)(2,1)}, bf16[112,768]{1,0:T(8,128)(2,1)}, u32[]{:S(2)}, u32[]{:S(2)}) collective-permute-start(bf16[112,768]{1,0:T(8,128)(2,1)} %get-tuple-element.242), channel_id=1, source_target_pairs={{0,3},{1,0},{2,1},{3,2},{4,7},{5,4},{6,5},{7,6},{8,11},{9,8},{10,9... | collective-permute-start | bytes 516104 | tf_op jit(solution)/shard_map/ppermute | solution.py:803
  (53 other events, 338.2 us)
Sparse Core Ops, SparseCore 0:
  14.5 65.6 all-gather.8
  117.2 61.1 all-gather.4
  184.7 85.6 all-gather.6

commit v2 on v1

--- a/solution.py
+++ b/solution.py
@@ -287,7 +287,14 @@
     chunk = n_z * feed_rows
     whole = fixed((rows, width))
     my_rows = pl.BlockSpec((rows, width), lambda j, info: (info[0], 0))
-    at = lambda j, info: info[3 + j]
+    numbers = [4 * side + number for side, number in chunks]
+
+    def at(j, info):
+        found = numbers[0]
+        for step, number in enumerate(numbers[1:], 1):
+            found = jnp.where(j >= step, number, found)
+        return found
+
     hidden_spec = pl.BlockSpec((chunk, rows), lambda j, info: (at(j, info), 0))
     slope_spec = pl.BlockSpec((rows, chunk), lambda j, info: (0, at(j, info)))
     in_specs = [
@@ -331,9 +338,6 @@
         scratch.append(pltpu.VMEM((rows, width), f32))
     else:
         shapes.append(((rows, width), f32, whole))
-    info = jnp.concatenate(
-        [info, jnp.array([4 * side + number for side, number in chunks], jnp.int32)]
-    )
     return pl.pallas_call(
         functools.partial(feed_forward_kernel, chunks, first is not None, last is not None),
         grid_spec=pltpu.PrefetchScalarGridSpec(
@@ -700,7 +704,7 @@
         other_refs, small_ref, rest = rest[:n_places], rest[n_places], rest[n_places + 1 :]
     out_refs, whole = rest[:-1], rest[-1]
     step = pl.program_id(0)
-    which = info_ref[step]
+    which = 2 * (info_ref[2] if adds else 1 - info_ref[2]) + step
     n_z, buckets, mine, _ = mixed_ref.shape
     count = mine // n_places
 
@@ -721,7 +725,7 @@
 
     for number in range(n_places):
         for s in range(n_z):
-            start = lax.rem(info_ref[2] + s, n_z) * mine + (info_ref[3] ^ number) * count
+            start = lax.rem(info_ref[0] + s, n_z) * mine + (info_ref[1] ^ number) * count
             value = whole[pl.ds(pl.multiple_of(start, 16), count), :]
             if adds:
                 value = value.astype(f32) + other_refs[number][s, 0].astype(f32)
@@ -740,13 +744,14 @@
     n_z, buckets = mixed.shape[:2]
     mine = width // n_z
     count = mine // n_places
+    side = lambda info: 1 - info[2] if other is None else info[2]
     by_step = pl.BlockSpec((n_z, 1, count, width), lambda i, info: (0, i, 0, 0))
     in_specs = [
         pl.BlockSpec(
-            (1, buckets, width, BUCKET), lambda i, info: (jnp.minimum(info[i], 2), 0, 0, 0)
+            (1, buckets, width, BUCKET), lambda i, info: (jnp.minimum(2 * side(info) + i, 2), 0, 0, 0)
         ),
         fixed((n_z, buckets, mine, BUCKET)),
-        pl.BlockSpec((rows, width), lambda i, info: (info[2], 0)),
+        pl.BlockSpec((rows, width), lambda i, info: (info[0], 0)),
         fixed((rows, width)),
     ]
     args = [grads, mixed, tokens, grad_attended]
@@ -981,6 +986,26 @@
         (first_normed, first_scale, vectors),
     )
     inner_came, outer_came = plane.swap(inner_go, 4), plane.swap(outer_go, 2)
+    grads, my_tokens_grad, back_sums = attend_back(
+        place_z, lengths, grad_attended, grad_first, attention_own, attention_remote, mixer,
+        *projected, key_mask_rows,
+    )
+    grads, inner_came, outer_came, output = together(grads, inner_came, outer_came, output)
+    inner_on, outer_on = (
+        plane.swap(add(inner_stay[1], inner_came[1]), 2),
+        plane.swap(add(outer_stay[1], outer_came[1]), 4),
+    )
+    tokens_grad = lax.all_gather(my_tokens_grad, "tensor", axis=0, tiled=True)
+
+    def weight_grads(other=None, small=None):
+        return attention_grads(n_places, info, grads, mixed, tokens, grad_attended, other, small)
+
+    sent = weight_grads()
+    sent, inner_on, outer_on, back_sums, first_sums, second_sums, bias_kept, bias_sent = together(
+        sent, inner_on, outer_on, back_sums, first_sums, second_sums, bias_kept, bias_sent
+    )
+    other = [plane.swap(part, 1) for part in sent]
+
     bias_grads = jnp.stack(
         [bias_kept[:, 0], bias_sent[:, 0]], axis=1
     )
@@ -997,29 +1022,6 @@
         axis=0,
     ).reshape(n_z, units)
 
-    grads, my_tokens_grad, back_sums = attend_back(
-        place_z, lengths, grad_attended, grad_first, attention_own, attention_remote, mixer,
-        *projected, key_mask_rows,
-    )
-    grads, inner_came, outer_came, output = together(grads, inner_came, outer_came, output)
-    inner_on, outer_on = (
-        plane.swap(add(inner_stay[1], inner_came[1]), 2),
-        plane.swap(add(outer_stay[1], outer_came[1]), 4),
-    )
-    tokens_grad = lax.all_gather(my_tokens_grad, "tensor", axis=0, tiled=True)
-
-    def weight_grads(side, other=None, small=None):
-        info = jnp.stack([2 * side, 2 * side + 1, z, place])
-        return attention_grads(
-            n_places, info, grads, mixed, tokens, grad_attended, other, small
-        )
-
-    sent = weight_grads(1 - core)
-    sent, inner_on, outer_on, back_sums, first_sums, second_sums, inner_bias_grad = together(
-        sent, inner_on, outer_on, back_sums, first_sums, second_sums, inner_bias_grad
-    )
-    other = [plane.swap(part, 1) for part in sent]
-
     small = jnp.concatenate(
         [first_sums[:3], second_sums[:3], inner_bias_grad, jnp.sum(back_sums, axis=0)[:2]], axis=0
     )
@@ -1027,7 +1029,7 @@
     small_rows = small.shape[0]
 
     small = add(small, plane.swap(small, 1))
-    kept = list(weight_grads(core, other, small))
+    kept = list(weight_grads(other, small))
     arrived = plane.to_places(kept)
     feed_parts = [
         jnp.concatenate(

time: 317 us -> 322 us (1.016)
  waiting for transfers between devices: 83.2 us -> 93.9 us
    ppermute x12, waiting for transfers between devices: 57.4 us -> 63.8 us  [shift(): return lax.ppermute(array, 'tensor', [(i, (i + by) % n) for i in range(n)])]
    ppermute x35, waiting for transfers between devices: 24.2 us -> 28.5 us  [swap(): return lax.ppermute(array, 'dp', [(i, i ^ bits) for i in range(self.n_dp)])]
  transfers between devices with their start and end apart: 51 -> 51, of which waited for: 24 -> 23; matrix products, arithmetic and copies ran while one was open for 11% -> 9% of each run, Pallas kernels for 39% -> 38%
where the time goes in v2:
time: 322 us; the launch traced here: 321 us
  Pallas kernels  123 us (38%)
  waiting for transfers between devices  93.9 us (29%)
  starting transfers between devices  50.3 us (16%)
  other arithmetic  24.1 us (7%)
  local copies, waits for them, and re-layouts  15.4 us (5%)
  between operations  14.6 us (5%)
    ppermute x12, waiting for transfers between devices, shift(): return lax.ppermute(array, 'tensor', [(i, (i + by) % n) for i in range(n)])  63.8 us
    pallas_call x2, Pallas kernels, feed_back(): pl.pallas_call(functools.partial(feed_back_kernel, keeps), grid_spec=pltp...  30.5 us
    ppermute x35, starting transfers between devices, swap(): return lax.ppermute(array, 'dp', [(i, i ^ bits) for i in range(self.n_dp)])  28.5 us
    ppermute x35, waiting for transfers between devices, swap(): return lax.ppermute(array, 'dp', [(i, i ^ bits) for i in range(self.n_dp)])  28.5 us
    pallas_call x2, Pallas kernels, feed_forward(): pl.pallas_call(functools.partial(feed_forward_kernel, chunks, first is no...  25.9 us
    pallas_call x1, Pallas kernels, attend_back(): pl.pallas_call(attend_back_kernel, grid_spec=pltpu.PrefetchScalarGridSpec...  22.4 us
    ppermute x12, starting transfers between devices, shift(): return lax.ppermute(array, 'tensor', [(i, (i + by) % n) for i in range(n)])  17.9 us
    pallas_call x2, Pallas kernels, attention_grads(): pl.pallas_call(functools.partial(attention_grads_kernel, n_places, other...  12.3 us
  transfers between devices with their start and end apart: 51, of which 23 were waited for; matrix products, arithmetic and copies ran while one was open for 9% of the time, Pallas kernels for 38%

profile of v2, /device:TPU:9, one launch (start us, length us, event | category | flops | bytes accessed | tf_op | source)
XLA Modules:
  0.0 321.0 jit_solution(15990009173741001517)
XLA Ops:
  15.1 11.8 %attend_forward.1 = bf16[4,1,208,512]{3,2,1,0:T(8,128)(2,1)} custom-call(s32[4,8]{1,0:T(4,128)} %lengths_ref.3, bf16[2048,768]{1,0:T(8,128)(2,1)} %tokens_ref.7, bf16[192,768]{1,0:T(8,128)(2,1)} %bitcast.165, bf16[192,768]{1,0:T(8,128)(2,1)} %bitcast.167, bf16[192,768]{1,0:T(8,128)(2,1)} %bitcast.169, bf16[16,512]{1,0:T(8,128)(2,1)} %reshape.150.biases_ref, ...), custom_call_target="tpu_custom_call" | custom-call | flops 3000000000 | bytes 3000000 | tf_op jit(solution)/shard_map/attend_forward/pallas_call | solution.py:121
  26.9 10.3 %collective-permute-done.1 = bf16[96,1536]{1,0:T(8,128)(2,1)S(1)} collective-permute-done((bf16[96,1536]{1,0:T(8,128)(2,1)S(1)}, bf16[96,1536]{1,0:T(8,128)(2,1)S(1)}, u32[]{:S(2)}, u32[]{:S(2)}) %collective-permute-start.1) | collective-permute-done | bytes 294944 | tf_op jit(solution)/shard_map/ppermute | solution.py:808
  37.2 2.9 collective-permute-done.2
  41.2 3.5 %all-to-all-start = ((bf16[4,1,208,512]{3,2,1,0:T(8,128)(2,1)}), bf16[4,1,208,512]{3,2,1,0:T(8,128)(2,1)S(1)}, u32[]{:S(2)}, u32[]{:S(2)}) async-start(bf16[4,1,208,512]{3,2,1,0:T(8,128)(2,1)} %attend_forward.1), calls=%async_computation | async-start | bytes 1703936 | tf_op jit(solution)/shard_map/all_to_all | solution.py:917
  52.6 2.8 pad_maximum_fusion.rest_2_.own_ref
  55.4 11.6 %collective-permute-done.3.rest_4_.rest_1_ = bf16[3,96,1536]{2,1,0:T(8,128)(2,1)} collective-permute-done((bf16[3,96,1536]{2,1,0:T(8,128)(2,1)}, bf16[3,96,1536]{2,1,0:T(8,128)(2,1)}, u32[]{:S(2)}, u32[]{:S(2)}) %collective-permute-start.3) | collective-permute-done | bytes 884768 | tf_op jit(solution)/shard_map/ppermute | solution.py:804
  73.4 2.8 collective-permute-done.6
  87.5 15.6 %feed_forward.2 = (bf16[3072,512]{1,0:T(8,128)(2,1)}, bf16[512,3072]{1,0:T(8,128)(2,1)}, bf16[512,768]{1,0:T(8,128)(2,1)}, f32[512,768]{1,0:T(8,128)}, f32[512,1]{1,0:T(8,128)}, /*index=5*/f32[512,768]{1,0:T(8,128)}) custom-call(s32[3]{0:T(128)} %pad_add_fusion.info_ref, f32[8,768]{1,0:T(8,128)} %convert_element_type.342.rest_0_.rest_9_, ...), custom_call_target="tpu_custom_call" | custom-call | flops 4499999744 | bytes 4500000 | tf_op jit(solution)/shard_map/feed_forward/pallas_call | solution.py:341
  105.0 2.7 collective-permute-done.16.rest_5_.rest_3_
  109.2 10.4 %feed_forward.3 = (bf16[3072,512]{1,0:T(8,128)(2,1)}, bf16[512,3072]{1,0:T(8,128)(2,1)}, bf16[512,768]{1,0:T(8,128)(2,1)}, f32[512,768]{1,0:T(8,128)}, bf16[512,768]{1,0:T(8,128)(2,1)}, /*index=5*/f32[8,768]{1,0:T(8,128)}) custom-call(s32[3]{0:T(128)} %pad_add_fusion.info_ref, ...), custom_call_target="tpu_custom_call", output_to_operand_aliasing={{0}: (10, {}), {1}: (11, {})} | custom-call | flops 1500000000 | bytes 1500000 | tf_op jit(solution)/shard_map/feed_forward/pallas_call | solution.py:341
  119.8 13.6 %feed_back.1 = (bf16[2,4,96,1536]{3,2,1,0:T(8,128)(2,1)}, bf16[2,4,96,1536]{3,2,1,0:T(8,128)(2,1)}, f32[4,1,384]{2,1,0:T(1,128)}, f32[512,768]{1,0:T(8,128)}) custom-call(s32[3]{0:T(128)} %pad_add_fusion.info_ref, bf16[512,768]{1,0:T(8,128)(2,1)} %get-tuple-element.145.grad_outer_ref, bf16[512,768]{1,0:T(8,128)(2,1)} %get-tuple-element.137.rest_7_.normed_low_ref, ...), custom_call_target="tpu_custom_call" | custom-call | flops 3000000000 | bytes 3000000 | tf_op jit(solution)/shard_map/feed_back/pallas_call | solution.py:470
  134.7 3.0 maximum_select_fusion
  137.7 6.7 %project.1 = (bf16[1,768,512]{2,1,0:T(8,128)(2,1)}, bf16[1,768,512]{2,1,0:T(8,128)(2,1)}, bf16[1,768,512]{2,1,0:T(8,128)(2,1)}) custom-call(s32[1]{0:T(128)} %bitcast.place_ref, bf16[2048,768]{1,0:T(8,128)(2,1)} %tokens_ref.7, bf16[192,2304]{1,0:T(8,128)(2,1)} %copy-done.3, bf16[3,192,2304]{2,1,0:T(8,128)(2,1)} %bitcast.143, ...), custom_call_target="tpu_custom_call" | custom-call | flops 1250000000 | bytes 1250000 | tf_op jit(solution)/shard_map/project/pallas_call | solution.py:557
  144.4 16.9 %feed_back_own.1 = (bf16[2,4,96,768]{3,2,1,0:T(8,128)(2,1)}, bf16[2,4,96,768]{3,2,1,0:T(8,128)(2,1)}, bf16[2,4,96,768]{3,2,1,0:T(8,128)(2,1)}, bf16[2,4,96,768]{...) custom-call(s32[3]{0:T(128)} %pad_add_fusion.info_ref, ...), custom_call_target="tpu_custom_call" | custom-call | flops 3000000000 | bytes 3000000 | tf_op jit(solution)/shard_map/feed_back_own/pallas_call | solution.py:470
  162.0 22.4 %attend_back.1 = (bf16[3,1,768,512]{3,2,1,0:T(8,128)(2,1)}, bf16[512,768]{1,0:T(8,128)(2,1)}, f32[1,8,768]{2,1,0:T(8,128)}) custom-call(s32[1]{0:T(128)} %bitcast.place_ref, s32[4,8]{1,0:T(4,128)} %lengths_ref.3, bf16[512,768]{1,0:T(8,128)(2,1)} %get-tuple-element.160.grad_attended_ref, f32[512,768]{1,0:T(8,128)} %get-tuple-element.161.grad_first_ref, ...), custom_call_target="tpu_custom_call" | custom-call | flops 5000000000 | bytes 5000000 | tf_op jit(solution)/shard_map/attend_back/pallas_call | solution.py:656
  184.4 4.4 %collective-permute-done.21 = bf16[2,4,96,768]{3,2,1,0:T(8,128)(2,1)} collective-permute-done((bf16[2,4,96,768]{3,2,1,0:T(8,128)(2,1)}, bf16[2,4,96,768]{3,2,1,0:T(8,128)(2,1)}, u32[]{:S(2)}, u32[]{:S(2)}) %collective-permute-start.21) | collective-permute-done | bytes 1179680 | tf_op jit(solution)/shard_map/ppermute | solution.py:804
  193.6 5.8 %attention_grads.2 = (bf16[4,2,48,768]{3,2,1,0:T(8,128)(2,1)}, bf16[4,2,48,768]{3,2,1,0:T(8,128)(2,1)}, bf16[4,2,48,768]{3,2,1,0:T(8,128)(2,1)}, bf16[4,2,48,768]{3,2,1,0:T(8,128)(2,1)}) custom-call(s32[3]{0:T(128)} %pad_add_fusion.info_ref, bf16[3,1,768,512]{3,2,1,0:T(8,128)(2,1)} %get-tuple-element.169.grads_ref, bf16[4,1,208,512]{3,2,1,0:T(8,128)(2,1)} %copy-done.2, ...), custom_call_target="tpu_custom_call" | custom-call | flops 125000000 | bytes 125000 | tf_op jit(solution)/shard_map/attention_grads/pallas_call | solution.py:765
  199.3 4.2 %collective-permute-done.24 = bf16[4,96,768]{2,1,0:T(8,128)(2,1)} collective-permute-done((bf16[4,96,768]{2,1,0:T(8,128)(2,1)S(1)}, bf16[4,96,768]{2,1,0:T(8,128)(2,1)}, u32[]{:S(2)}, u32[]{:S(2)}) %collective-permute-start.24) | collective-permute-done | bytes 589856 | tf_op jit(solution)/shard_map/ppermute | solution.py:804
  203.6 3.1 collective-permute-done.23
  209.2 2.8 collective-permute-start.29
  216.6 2.1 collective-permute-start.37
  222.7 6.6 %attention_grads.3 = (bf16[400,768]{1,0:T(8,128)(2,1)}, bf16[400,768]{1,0:T(8,128)(2,1)}, bf16[400,768]{1,0:T(8,128)(2,1)}, bf16[400,768]{1,0:T(8,128)(2,1)}) custom-call(s32[3]{0:T(128)} %pad_add_fusion.info_ref, bf16[3,1,768,512]{3,2,1,0:T(8,128)(2,1)} %get-tuple-element.169.grads_ref, bf16[4,1,208,512]{3,2,1,0:T(8,128)(2,1)} %copy-done.2, ...), custom_call_target="tpu_custom_call" | custom-call | flops 125000000 | bytes 125000 | tf_op jit(solution)/shard_map/attention_grads/pallas_call | solution.py:765
  231.3 11.5 %collective-permute-done.36 = bf16[96,1536]{1,0:T(8,128)(2,1)S(1)} collective-permute-done((bf16[96,1536]{1,0:T(8,128)(2,1)S(1)}, bf16[96,1536]{1,0:T(8,128)(2,1)S(1)}, u32[]{:S(2)}, u32[]{:S(2)}) %collective-permute-start.36) | collective-permute-done | bytes 294944 | tf_op jit(solution)/shard_map/ppermute | solution.py:808
  243.9 4.2 %copied.2 = bf16[2048,768]{1,0:T(8,128)(2,1)} custom-call(bf16[2048,768]{1,0:T(8,128)(2,1)} %all-gather.5.cloned.1.call-done.from_ref), custom_call_target="tpu_custom_call" | custom-call | flops 125000000 | bytes 125000 | tf_op jit(solution)/shard_map/copied/pallas_call | solution.py:526
  248.1 4.3 %collective-permute-done.37 = bf16[96,1536]{1,0:T(8,128)(2,1)S(1)} collective-permute-done((bf16[96,1536]{1,0:T(8,128)(2,1)S(1)}, bf16[96,1536]{1,0:T(8,128)(2,1)S(1)}, u32[]{:S(2)}, u32[]{:S(2)}) %collective-permute-start.37) | collective-permute-done | bytes 294944 | tf_op jit(solution)/shard_map/ppermute | solution.py:808
  252.4 21.3 %collective-permute-done.38 = bf16[96,1536]{1,0:T(8,128)(2,1)S(1)} collective-permute-done((bf16[96,1536]{1,0:T(8,128)(2,1)S(1)}, bf16[96,1536]{1,0:T(8,128)(2,1)S(1)}, u32[]{:S(2)}, u32[]{:S(2)}) %collective-permute-start.38) | collective-permute-done | bytes 294944 | tf_op jit(solution)/shard_map/ppermute | solution.py:808
  277.8 2.3 collective-permute-start.33
  280.1 2.9 collective-permute-start.34
  284.8 4.2 %copied.3 = bf16[2048,768]{1,0:T(8,128)(2,1)} custom-call(bf16[2048,768]{1,0:T(8,128)(2,1)} %all-gather.7.cloned.1.call-done.from_ref), custom_call_target="tpu_custom_call" | custom-call | flops 125000000 | bytes 125000 | tf_op jit(solution)/shard_map/copied/pallas_call | solution.py:526
  289.7 4.8 %collective-permute-done.34 = bf16[112,768]{1,0:T(8,128)(2,1)S(1)} collective-permute-done((bf16[112,768]{1,0:T(8,128)(2,1)}, bf16[112,768]{1,0:T(8,128)(2,1)S(1)}, u32[]{:S(2)}, u32[]{:S(2)}) %collective-permute-start.34) | collective-permute-done | bytes 172064 | tf_op jit(solution)/shard_map/ppermute | solution.py:808
  294.5 2.8 collective-permute-done.35
  304.8 4.7 %finish_feed.1 = (f32[768,768]{1,0:T(8,128)}, f32[768,768]{1,0:T(8,128)}) custom-call(s32[1]{0:T(128)} %bitcast.2.core_ref, bf16[4,96,1536]{2,1,0:T(8,128)(2,1)} %bitcast.156, bf16[4,96,1536]{2,1,0:T(8,128)(2,1)} %collective-permute-done.45.other_ref), custom_call_target="tpu_custom_call" | custom-call | flops 1250000000 | bytes 1250000 | tf_op jit(solution)/shard_map/finish_feed/pallas_call | solution.py:501
  (240 shorter events, 77.7 us)
Async XLA Ops:
  7.2 73.0 %all-gather.9.cloned.1.call-start = ((), (), s32[]{:S(2)}) async-start(), calls=%async_computation.3 | async-start | bytes 1216512 | tf_op jit(solution)/shard_map/all_gather | solution.py:812
  10.5 16.4 %collective-permute-start = (bf16[96,1536]{1,0:T(8,128)(2,1)S(1)}, bf16[96,1536]{1,0:T(8,128)(2,1)S(1)}, u32[]{:S(2)}, u32[]{:S(2)}) collective-permute-start(bf16[96,1536]{1,0:T(8,128)(2,1)S(1)} %pad_maximum_fusion.7), channel_id=1, source_target_pairs={{0,1},{1,2},{2,3},{3,0},{4,5},{5,6},{6,7},{7,4},{8,9},{9,10},{10,1... | collective-permute-start | bytes 884744 | tf_op jit(solution)/shard_map/ppermute | solution.py:808
  11.8 25.4 %collective-permute-start.1 = (bf16[96,1536]{1,0:T(8,128)(2,1)S(1)}, bf16[96,1536]{1,0:T(8,128)(2,1)S(1)}, u32[]{:S(2)}, u32[]{:S(2)}) collective-permute-start(bf16[96,1536]{1,0:T(8,128)(2,1)S(1)} %pad_maximum_fusion.7), channel_id=1, source_target_pairs={{0,2},{1,3},{2,0},{3,1},{4,6},{5,7},{6,4},{7,5},{8,10},{9,11},{10,... | collective-permute-start | bytes 884744 | tf_op jit(solution)/shard_map/ppermute | solution.py:808
  12.9 27.3 %collective-permute-start.2 = (bf16[96,1536]{1,0:T(8,128)(2,1)S(1)}, bf16[96,1536]{1,0:T(8,128)(2,1)S(1)}, u32[]{:S(2)}, u32[]{:S(2)}) collective-permute-start(bf16[96,1536]{1,0:T(8,128)(2,1)S(1)} %pad_maximum_fusion.7), channel_id=1, source_target_pairs={{0,3},{1,0},{2,1},{3,2},{4,7},{5,4},{6,5},{7,6},{8,11},{9,8},{10,9... | collective-permute-start | bytes 884744 | tf_op jit(solution)/shard_map/ppermute | solution.py:808
  41.2 30.7 %all-to-all-start = ((bf16[4,1,208,512]{3,2,1,0:T(8,128)(2,1)}), bf16[4,1,208,512]{3,2,1,0:T(8,128)(2,1)S(1)}, u32[]{:S(2)}, u32[]{:S(2)}) async-start(bf16[4,1,208,512]{3,2,1,0:T(8,128)(2,1)} %attend_forward.1), calls=%async_computation | async-start | bytes 1703936 | tf_op jit(solution)/shard_map/all_to_all | solution.py:917
  44.8 144.1 %all-gather.5.cloned.1.call-start = ((), (), s32[]{:S(2)}) async-start(), calls=%async_computation.1 | async-start | bytes 3932160 | tf_op jit(solution)/shard_map/all_gather | solution.py:969
  44.8 22.2 %collective-permute-start.3 = (bf16[3,96,1536]{2,1,0:T(8,128)(2,1)}, bf16[3,96,1536]{2,1,0:T(8,128)(2,1)}, u32[]{:S(2)}, u32[]{:S(2)}) collective-permute-start(bf16[3,96,1536]{2,1,0:T(8,128)(2,1)} %pad_maximum_fusion.3.rest_3_.rest_0_), channel_id=1, source_target_pairs={{0,8},{4,12},{8,0},{12,4},{16,24},{20,28},{24,16},{28,20},{1,9},{5... | collective-permute-start | bytes 2654216 | tf_op jit(solution)/shard_map/ppermute | solution.py:804
  46.1 23.3 %collective-permute-start.4 = (bf16[3,96,1536]{2,1,0:T(8,128)(2,1)}, bf16[3,96,1536]{2,1,0:T(8,128)(2,1)}, u32[]{:S(2)}, u32[]{:S(2)}) collective-permute-start(bf16[3,96,1536]{2,1,0:T(8,128)(2,1)} %pad_maximum_fusion.3.rest_3_.rest_0_), channel_id=1, source_target_pairs={{0,16},{4,20},{8,24},{12,28},{16,0},{20,4},{24,8},{28,12},{1,17},{... | collective-permute-start | bytes 2654216 | tf_op jit(solution)/shard_map/ppermute | solution.py:804
  48.4 25.0 %collective-permute-start.5 = (bf16[24,2304]{1,0:T(8,128)(2,1)S(1)}, bf16[24,2304]{1,0:T(8,128)(2,1)S(1)}, u32[]{:S(2)}, u32[]{:S(2)}) collective-permute-start(bf16[24,2304]{1,0:T(8,128)(2,1)S(1)} %constant_dynamic-slice_fusion.1), channel_id=1, source_target_pairs={{0,1},{1,2},{2,3},{3,0},{4,5},{5,6},{6,7},{7,4},{8,9},{9,10},{10,1... | collective-permute-start | bytes 331784 | tf_op jit(solution)/shard_map/ppermute | solution.py:808
  48.8 27.3 %collective-permute-start.6 = (bf16[24,2304]{1,0:T(8,128)(2,1)S(1)}, bf16[24,2304]{1,0:T(8,128)(2,1)S(1)}, u32[]{:S(2)}, u32[]{:S(2)}) collective-permute-start(bf16[24,2304]{1,0:T(8,128)(2,1)S(1)} %constant_dynamic-slice_fusion.1), channel_id=1, source_target_pairs={{0,2},{1,3},{2,0},{3,1},{4,6},{5,7},{6,4},{7,5},{8,10},{9,11},{10,... | collective-permute-start | bytes 331784 | tf_op jit(solution)/shard_map/ppermute | solution.py:808
  49.8 28.2 %collective-permute-start.7 = (bf16[24,2304]{1,0:T(8,128)(2,1)S(1)}, bf16[24,2304]{1,0:T(8,128)(2,1)S(1)}, u32[]{:S(2)}, u32[]{:S(2)}) collective-permute-start(bf16[24,2304]{1,0:T(8,128)(2,1)S(1)} %constant_dynamic-slice_fusion.1), channel_id=1, source_target_pairs={{0,3},{1,0},{2,1},{3,2},{4,7},{5,4},{6,5},{7,6},{8,11},{9,8},{10,9... | collective-permute-start | bytes 331784 | tf_op jit(solution)/shard_map/ppermute | solution.py:808
  68.1 35.0 %collective-permute-start.11 = (bf16[3,48,1536]{2,1,0:T(8,128)(2,1)S(1)}, bf16[3,48,1536]{2,1,0:T(8,128)(2,1)S(1)}, u32[]{:S(2)}, u32[]{:S(2)}) collective-permute-start(bf16[3,48,1536]{2,1,0:T(8,128)(2,1)S(1)} %slice.349), channel_id=1, source_target_pairs={{0,16},{4,20},{8,24},{12,28},{16,0},{20,4},{24,8},{28,12},{1,17},{... | collective-permute-start | bytes 1327112 | tf_op jit(solution)/shard_map/ppermute | solution.py:804
  71.2 31.9 %collective-permute-start.12 = (bf16[3,48,1536]{2,1,0:T(8,128)(2,1)}, bf16[3,48,1536]{2,1,0:T(8,128)(2,1)S(1)}, u32[]{:S(2)}, u32[]{:S(2)}) collective-permute-start(bf16[3,48,1536]{2,1,0:T(8,128)(2,1)} %slice.350), channel_id=1, source_target_pairs={{0,8},{4,12},{8,0},{12,4},{16,24},{20,28},{24,16},{28,20},{1,9},{5... | collective-permute-start | bytes 1327112 | tf_op jit(solution)/shard_map/ppermute | solution.py:804
  82.8 20.3 %collective-permute-start.13 = (bf16[3,24,2304]{2,1,0:T(8,128)(2,1)S(1)}, bf16[3,24,2304]{2,1,0:T(8,128)(2,1)S(1)}, u32[]{:S(2)}, u32[]{:S(2)}) collective-permute-start(bf16[3,24,2304]{2,1,0:T(8,128)(2,1)S(1)} %get-tuple-element.243), channel_id=1, source_target_pairs={{0,8},{4,12},{8,0},{12,4},{16,24},{20,28},{24,16},{28,20},{1,9},{5... | collective-permute-start | bytes 995336 | tf_op jit(solution)/shard_map/ppermute | solution.py:804
  84.2 18.9 %collective-permute-start.14 = (bf16[3,24,2304]{2,1,0:T(8,128)(2,1)S(1)}, bf16[3,24,2304]{2,1,0:T(8,128)(2,1)S(1)}, u32[]{:S(2)}, u32[]{:S(2)}) collective-permute-start(bf16[3,24,2304]{2,1,0:T(8,128)(2,1)S(1)} %get-tuple-element.243), channel_id=1, source_target_pairs={{0,16},{4,20},{8,24},{12,28},{16,0},{20,4},{24,8},{28,12},{1,17},{... | collective-permute-start | bytes 995336 | tf_op jit(solution)/shard_map/ppermute | solution.py:804
  85.5 17.6 %collective-permute-start.15 = (bf16[3,24,2304]{2,1,0:T(8,128)(2,1)S(1)}, bf16[3,24,2304]{2,1,0:T(8,128)(2,1)S(1)}, u32[]{:S(2)}, u32[]{:S(2)}) collective-permute-start(bf16[3,24,2304]{2,1,0:T(8,128)(2,1)S(1)} %get-tuple-element.243), channel_id=1, source_target_pairs={{0,24},{4,28},{8,16},{12,20},{16,8},{20,12},{24,0},{28,4},{1,25},{... | collective-permute-start | bytes 995336 | tf_op jit(solution)/shard_map/ppermute | solution.py:804
  103.9 16.0 %collective-permute-start.18 = (bf16[4,3,24,2304]{3,2,0,1:T(8,128)(2,1)S(1)}, bf16[4,3,24,2304]{3,2,0,1:T(8,128)(2,1)}, u32[]{:S(2)}, u32[]{:S(2)}) collective-permute-start(bf16[4,3,24,2304]{3,2,0,1:T(8,128)(2,1)S(1)} %bitcast.147), channel_id=1, source_target_pairs={{0,4},{4,0},{8,12},{12,8},{16,20},{20,16},{24,28},{28,24},{1,5},{5... | collective-permute-start | bytes 3981320 | tf_op jit(solution)/shard_map/ppermute | solution.py:804
  119.5 165.3 %all-gather.7.cloned.1.call-start = ((), (), s32[]{:S(2)}) async-start(), calls=%async_computation.2 | async-start | bytes 3932160 | tf_op jit(solution)/shard_map/all_gather | solution.py:998
  161.2 27.6 %collective-permute-start.21 = (bf16[2,4,96,768]{3,2,1,0:T(8,128)(2,1)}, bf16[2,4,96,768]{3,2,1,0:T(8,128)(2,1)}, u32[]{:S(2)}, u32[]{:S(2)}) collective-permute-start(bf16[2,4,96,768]{3,2,1,0:T(8,128)(2,1)} %get-tuple-element.166), channel_id=1, source_target_pairs={{0,16},{4,20},{8,24},{12,28},{16,0},{20,4},{24,8},{28,12},{1,17},{... | collective-permute-start | bytes 3538952 | tf_op jit(solution)/shard_map/ppermute | solution.py:804
  161.7 27.2 %collective-permute-start.22 = (bf16[2,4,96,768]{3,2,1,0:T(8,128)(2,1)}, bf16[2,4,96,768]{3,2,1,0:T(8,128)(2,1)}, u32[]{:S(2)}, u32[]{:S(2)}) collective-permute-start(bf16[2,4,96,768]{3,2,1,0:T(8,128)(2,1)} %get-tuple-element.167), channel_id=1, source_target_pairs={{0,8},{4,12},{8,0},{12,4},{16,24},{20,28},{24,16},{28,20},{1,9},{5... | collective-permute-start | bytes 3538952 | tf_op jit(solution)/shard_map/ppermute | solution.py:804
  190.1 13.5 %collective-permute-start.24 = (bf16[4,96,768]{2,1,0:T(8,128)(2,1)S(1)}, bf16[4,96,768]{2,1,0:T(8,128)(2,1)}, u32[]{:S(2)}, u32[]{:S(2)}) collective-permute-start(bf16[4,96,768]{2,1,0:T(8,128)(2,1)S(1)} %fusion.5), channel_id=1, source_target_pairs={{0,16},{4,20},{8,24},{12,28},{16,0},{20,4},{24,8},{28,12},{1,17},{... | collective-permute-start | bytes 1769480 | tf_op jit(solution)/shard_map/ppermute | solution.py:804
  193.3 13.4 %collective-permute-start.23 = (bf16[4,96,768]{2,1,0:T(8,128)(2,1)}, bf16[4,96,768]{2,1,0:T(8,128)(2,1)}, u32[]{:S(2)}, u32[]{:S(2)}) collective-permute-start(bf16[4,96,768]{2,1,0:T(8,128)(2,1)} %fusion.4), channel_id=1, source_target_pairs={{0,8},{4,12},{8,0},{12,4},{16,24},{20,28},{24,16},{28,20},{1,9},{5... | collective-permute-start | bytes 1769480 | tf_op jit(solution)/shard_map/ppermute | solution.py:804
  216.2 26.6 %collective-permute-start.36 = (bf16[96,1536]{1,0:T(8,128)(2,1)S(1)}, bf16[96,1536]{1,0:T(8,128)(2,1)S(1)}, u32[]{:S(2)}, u32[]{:S(2)}) collective-permute-start(bf16[96,1536]{1,0:T(8,128)(2,1)S(1)} %pad_maximum_fusion.8), channel_id=1, source_target_pairs={{0,3},{1,0},{2,1},{3,2},{4,7},{5,4},{6,5},{7,6},{8,11},{9,8},{10,9... | collective-permute-start | bytes 884744 | tf_op jit(solution)/shard_map/ppermute | solution.py:808
  216.6 35.8 %collective-permute-start.37 = (bf16[96,1536]{1,0:T(8,128)(2,1)S(1)}, bf16[96,1536]{1,0:T(8,128)(2,1)S(1)}, u32[]{:S(2)}, u32[]{:S(2)}) collective-permute-start(bf16[96,1536]{1,0:T(8,128)(2,1)S(1)} %pad_maximum_fusion.9), channel_id=1, source_target_pairs={{0,2},{1,3},{2,0},{3,1},{4,6},{5,7},{6,4},{7,5},{8,10},{9,11},{10,... | collective-permute-start | bytes 884744 | tf_op jit(solution)/shard_map/ppermute | solution.py:808
  218.7 55.1 %collective-permute-start.38 = (bf16[96,1536]{1,0:T(8,128)(2,1)S(1)}, bf16[96,1536]{1,0:T(8,128)(2,1)S(1)}, u32[]{:S(2)}, u32[]{:S(2)}) collective-permute-start(bf16[96,1536]{1,0:T(8,128)(2,1)S(1)} %pad_maximum_fusion.10), channel_id=1, source_target_pairs={{0,1},{1,2},{2,3},{3,0},{4,5},{5,6},{6,7},{7,4},{8,9},{9,10},{10,1... | collective-permute-start | bytes 884744 | tf_op jit(solution)/shard_map/ppermute | solution.py:808
  229.3 47.3 %collective-permute-start.30 = (bf16[400,768]{1,0:T(8,128)(2,1)}, bf16[400,768]{1,0:T(8,128)(2,1)S(1)}, u32[]{:S(2)}, u32[]{:S(2)}) collective-permute-start(bf16[400,768]{1,0:T(8,128)(2,1)} %get-tuple-element.192), channel_id=1, source_target_pairs={{0,8},{4,12},{8,0},{12,4},{16,24},{20,28},{24,16},{28,20},{1,9},{5... | collective-permute-start | bytes 1843208 | tf_op jit(solution)/shard_map/ppermute | solution.py:804
  230.2 46.5 %collective-permute-start.31 = (bf16[400,768]{1,0:T(8,128)(2,1)}, bf16[400,768]{1,0:T(8,128)(2,1)S(1)}, u32[]{:S(2)}, u32[]{:S(2)}) collective-permute-start(bf16[400,768]{1,0:T(8,128)(2,1)} %get-tuple-element.193), channel_id=1, source_target_pairs={{0,16},{4,20},{8,24},{12,28},{16,0},{20,4},{24,8},{28,12},{1,17},{... | collective-permute-start | bytes 1843208 | tf_op jit(solution)/shard_map/ppermute | solution.py:804
  242.8 33.9 %collective-permute-start.32 = (bf16[400,768]{1,0:T(8,128)(2,1)}, bf16[400,768]{1,0:T(8,128)(2,1)S(1)}, u32[]{:S(2)}, u32[]{:S(2)}) collective-permute-start(bf16[400,768]{1,0:T(8,128)(2,1)} %get-tuple-element.194), channel_id=1, source_target_pairs={{0,24},{4,28},{8,16},{12,20},{16,8},{20,12},{24,0},{28,4},{1,25},{... | collective-permute-start | bytes 1843208 | tf_op jit(solution)/shard_map/ppermute | solution.py:804
  275.4 13.6 %collective-permute-start.40 = (bf16[96,1536]{1,0:T(8,128)(2,1)S(1)}, bf16[96,1536]{1,0:T(8,128)(2,1)S(1)}, u32[]{:S(2)}, u32[]{:S(2)}) collective-permute-start(bf16[96,1536]{1,0:T(8,128)(2,1)S(1)} %add_convert_fusion.2), channel_id=1, source_target_pairs={{0,16},{4,20},{8,24},{12,28},{16,0},{20,4},{24,8},{28,12},{1,17},{... | collective-permute-start | bytes 884744 | tf_op jit(solution)/shard_map/ppermute | solution.py:804
  276.6 13.0 %collective-permute-start.41 = (bf16[96,1536]{1,0:T(8,128)(2,1)S(1)}, bf16[96,1536]{1,0:T(8,128)(2,1)S(1)}, u32[]{:S(2)}, u32[]{:S(2)}) collective-permute-start(bf16[96,1536]{1,0:T(8,128)(2,1)S(1)} %add_convert_fusion.2), channel_id=1, source_target_pairs={{0,24},{4,28},{8,16},{12,20},{16,8},{20,12},{24,0},{28,4},{1,25},{... | collective-permute-start | bytes 884744 | tf_op jit(solution)/shard_map/ppermute | solution.py:804
  280.1 14.4 %collective-permute-start.34 = (bf16[112,768]{1,0:T(8,128)(2,1)}, bf16[112,768]{1,0:T(8,128)(2,1)S(1)}, u32[]{:S(2)}, u32[]{:S(2)}) collective-permute-start(bf16[112,768]{1,0:T(8,128)(2,1)} %get-tuple-element.245), channel_id=1, source_target_pairs={{0,2},{1,3},{2,0},{3,1},{4,6},{5,7},{6,4},{7,5},{8,10},{9,11},{10,... | collective-permute-start | bytes 516104 | tf_op jit(solution)/shard_map/ppermute | solution.py:808
  282.9 14.3 %collective-permute-start.35 = (bf16[112,768]{1,0:T(8,128)(2,1)}, bf16[112,768]{1,0:T(8,128)(2,1)}, u32[]{:S(2)}, u32[]{:S(2)}) collective-permute-start(bf16[112,768]{1,0:T(8,128)(2,1)} %get-tuple-element.244), channel_id=1, source_target_pairs={{0,3},{1,0},{2,1},{3,2},{4,7},{5,4},{6,5},{7,6},{8,11},{9,8},{10,9... | collective-permute-start | bytes 516104 | tf_op jit(solution)/shard_map/ppermute | solution.py:808
  (52 other events, 351.7 us)
Sparse Core Ops, SparseCore 0:
  14.5 65.6 all-gather.8
  119.7 61.0 all-gather.4
  193.6 86.5 all-gather.6
